TPU v7x, 768 devices: a whole 4x8x12 slice. The times are simulated.
768 devices in a mesh: dp: 96 (over y_hi, z, core), ep: 8 (over x, y_lo).
Axes of the slice: x: 4, y: 8 (y_hi: 4, y_lo: 2; y = y_hi * 2 + y_lo), z: 12, core: 2. Of those that a mesh axis runs over, the one named last changes fastest.
Arguments:
- grad_out: bfloat16 [12288, 6144], P('dp', 'ep'), may hold values from -6 to 6
- expert_ids: int32 [12288, 4], P('dp'), may hold values from 0 to 15, all different within a row
- route_probs: float32 [12288, 4], P('dp'), may hold values from 0.1 to 0.9
- saved_inputs: bfloat16 [1536, 6144], P(None, 'ep'), may hold values from -6 to 6
- w_gate: bfloat16 [10752, 6144], P('dp', 'ep'), may hold values from -0.078125 to 0.078125
- w_up: bfloat16 [10752, 6144], P('dp', 'ep'), may hold values from -0.078125 to 0.078125
- w_down: bfloat16 [10752, 6144], P('dp', 'ep'), may hold values from -0.3125 to 0.3125
Outputs:
- grad_in: bfloat16 [12288, 6144], P('dp', 'ep')
- grad_gate: float32 [10752, 6144], P('dp', 'ep')
- grad_up: float32 [10752, 6144], P('dp', 'ep')
- grad_down: float32 [10752, 6144], P('dp', 'ep')
All inputs are finite; a program needn't handle non-finite values.
Results may differ from a plain program's by a relative error of at most 0.012.
Values may be sent and summed in bfloat16 or wider, within the bound.
No kernel may reach another device: no remote copies, remote signals or barrier semaphores. Data moves between devices by JAX's collectives and lax.ppermute only.
A program may use at most 32 MiB of HBM per device.

v0:
```python
import jax
import jax.numpy as jnp
from jax import lax
from jax.sharding import PartitionSpec as P


def route_block(routes, chances, capacity):
    matches = routes == 0
    chosen = jnp.any(matches, axis=1).astype(jnp.int32)
    weight = jnp.sum(jnp.where(matches, chances, jnp.zeros_like(chances)), axis=1)
    earlier = jnp.cumsum(chosen) - chosen
    retained = (chosen > 0) & (earlier < capacity)
    placement = (
        (earlier[None, :] == jnp.arange(capacity, dtype=jnp.int32)[:, None]) & retained[None, :]
    ).astype(jnp.float32)
    return (placement, weight)


def local(grad_out, expert_ids, route_probs, saved_inputs, w_gate, w_up, w_down):
    capacity = grad_out.shape[0] // 8
    placement, weight = route_block(expert_ids, route_probs, capacity)
    residual = grad_out.astype(jnp.float32)
    weighted = weight[:, None] * residual
    outgoing = jnp.dot(placement, weighted, precision=lax.Precision.HIGHEST).astype(jnp.bfloat16)
    gate_part = jnp.dot(saved_inputs, w_gate.T, preferred_element_type=jnp.float32)
    up_part = jnp.dot(saved_inputs, w_up.T, preferred_element_type=jnp.float32)
    gathered = lax.all_gather(outgoing, "dp", axis=0, tiled=True)
    hid_part = jnp.dot(gathered, w_down.T, preferred_element_type=jnp.float32)
    gate_pre, up_pre, hid_grad = lax.psum((gate_part, up_part, hid_part), "ep")
    sigmoid_gate = jax.nn.sigmoid(gate_pre)
    activated = gate_pre * sigmoid_gate
    hidden = (activated * up_pre).astype(jnp.bfloat16)
    gate_slope = sigmoid_gate + gate_pre * sigmoid_gate * (1.0 - sigmoid_gate)
    gate_grad = (hid_grad * up_pre * gate_slope).astype(jnp.bfloat16)
    up_grad = (hid_grad * activated).astype(jnp.bfloat16)
    grad_gate = jnp.dot(gate_grad.T, saved_inputs, preferred_element_type=jnp.float32)
    grad_up = jnp.dot(up_grad.T, saved_inputs, preferred_element_type=jnp.float32)
    grad_down = jnp.dot(hidden.T, gathered, preferred_element_type=jnp.float32)
    own_slots = lax.psum_scatter(
        jnp.dot(gate_grad, w_gate, preferred_element_type=jnp.float32)
        + jnp.dot(up_grad, w_up, preferred_element_type=jnp.float32),
        "dp",
        scatter_dimension=0,
        tiled=True,
    ).astype(jnp.bfloat16)
    routed = jnp.dot(placement.T, own_slots.astype(jnp.float32), precision=lax.Precision.HIGHEST)
    grad_in = (residual + routed).astype(jnp.bfloat16)
    return (grad_in, grad_gate, grad_up, grad_down)


def solution(mesh):
    in_specs = (
        P("dp", "ep"),
        P("dp", None),
        P("dp", None),
        P(None, "ep"),
        P("dp", "ep"),
        P("dp", "ep"),
        P("dp", "ep"),
    )
    out_specs = (P("dp", "ep"), P("dp", "ep"), P("dp", "ep"), P("dp", "ep"))
    return jax.shard_map(local, mesh=mesh, in_specs=in_specs, out_specs=out_specs, check_vma=False)
```

profile of v0, /device:TPU:4, one launch (start us, length us, event | category | flops | bytes accessed | tf_op | source)
XLA Modules:
  0.0 489.2 jit_solution(7195827651933042308)
XLA Ops:
  7.2 0.0 all-gather.2.cloned.1.call-start
  7.2 0.9 fusion.13
  8.1 0.1 copy.12
  8.2 0.2 reduce-window.7
  8.4 0.1 reduce
  8.5 0.7 select_reduce_fusion
  9.2 1.9 convolution_convert_fusion
  11.1 0.0 all-gather.2.cloned.1.call-update
  11.1 0.0 all-reduce.3.cloned.1.call-start
  11.2 2.7 fusion.16
  13.9 1.7 fusion.15
  15.6 120.7 %all-gather.2.cloned.1.call-done = bf16[1536,768]{1,0:T(8,128)(2,1)} async-done(((bf16[16,768]{1,0:T(8,128)(2,1)}), bf16[1536,768]{1,0:T(8,128)(2,1)}) %all-gather.2.cloned.1.call-update) | async-done | bytes 2359312 | tf_op jit(solution)/shard_map/all_gather | solution.py:27
  136.2 3.4 fusion.14
  139.6 0.0 all-reduce.3.cloned.1.call-update
  139.6 0.0 reduce-scatter.2.cloned.1.call-start
  139.7 115.1 %all-reduce.3.cloned.1.call-done = (f32[1536,112]{0,1:T(8,128)}, f32[1536,112]{0,1:T(8,128)}, f32[1536,112]{0,1:T(8,128)}) async-done(((f32[1536,112]{0,1:T(8,128)}, f32[1536,112]{0,1:T(8,128)}, f32[1536,112]{0,1:T(8,128)}), (f32[1536,112]{0,1:T(8,128)}, f32[1536,112]{0,1:T(8,128)}, f32[1536,112]{0,1:T(8,128)})) %all-reduce.3.cloned.1.call-update) | async-done | bytes 2064400 | tf_op jit(solution)/shard_map/psum | solution.py:29
  254.8 1.8 multiply_convert_fusion.1
  256.6 0.8 fusion.17
  257.4 2.9 convolution_add_fusion
  260.4 1.2 fusion.19
  261.7 1.2 fusion.18
  262.9 1.3 fusion.2
  264.2 216.8 %reduce-scatter.2.cloned.1.call-done = f32[16,768]{1,0:T(8,128)} async-done(((f32[1536,768]{1,0:T(8,128)}), f32[16,768]{1,0:T(8,128)}) %reduce-scatter.2.cloned.1.call-update) | async-done | bytes 49168 | tf_op jit(solution)/shard_map/reduce_scatter | solution.py:39
  481.0 1.7 fusion
  (20 shorter events, 0.1 us)
Async XLA Ops:
  7.2 4.0 copy-start
  7.2 129.1 %all-gather.2.cloned.1.call-start = ((), (), s32[]{:S(2)}) async-start(), calls=%async_computation.1 | async-start | bytes 2383872 | tf_op jit(solution)/shard_map/all_gather | solution.py:27
  11.1 2.7 copy-start.6
  11.1 243.7 %all-reduce.3.cloned.1.call-start = ((), (), s32[]{:S(2)}) async-start(), calls=%async_computation.3 | async-start | bytes 4128768 | tf_op jit(solution)/shard_map/psum | solution.py:29
  13.9 122.4 %copy-start.7 = (bf16[112,768]{1,0:T(8,128)(2,1)S(1)}, bf16[112,768]{1,0:T(8,128)(2,1)}, u32[]{:S(2)}) copy-start(bf16[112,768]{1,0:T(8,128)(2,1)} %param.13) | copy-start | bytes 516100
  139.6 117.0 %copy-start.3 = (bf16[112,768]{1,0:T(8,128)(2,1)S(1)}, bf16[112,768]{1,0:T(8,128)(2,1)}, u32[]{:S(2)}) copy-start(bf16[112,768]{1,0:T(8,128)(2,1)} %param.11) | copy-start | bytes 516100
  139.6 341.3 %reduce-scatter.2.cloned.1.call-start = ((), (), s32[]{:S(2)}) async-start(), calls=%async_computation.2 | async-start | bytes 4767744 | tf_op jit(solution)/shard_map/reduce_scatter | solution.py:39
  260.4 2.5 copy-start.1
  260.4 2.5 copy-start.4
  260.4 2.5 copy-start.5
  262.9 218.1 %copy-start.2 = (bf16[128,768]{1,0:T(8,128)(2,1)S(1)}, bf16[128,768]{1,0:T(8,128)(2,1)}, u32[]{:S(2)}) copy-start(bf16[128,768]{1,0:T(8,128)(2,1)} %param.7) | copy-start | bytes 589828
Sparse Core Ops, SparseCore 0:
  12.3 123.9 all-gather.1
  139.8 114.9 all-reduce.2
  260.5 220.3 reduce-scatter.1
where the time goes:
time: 490 us; the launch traced here: 489 us
  waiting for transfers between devices  453 us (92%)
  matrix products  18.9 us (4%)
  between operations  13.8 us (3%)
    reduce_scatter x1, waiting for transfers between devices, local(): lax.psum_scatter(jnp.dot(gate_grad, w_gate, preferred_element_type=jnp.fl...  217 us
    all_gather x1, waiting for transfers between devices, local(): gathered = lax.all_gather(outgoing, 'dp', axis=0, tiled=True)  121 us
    psum x1, waiting for transfers between devices, local(): gate_pre, up_pre, hid_grad = lax.psum((gate_part, up_part, hid_part), 'ep')  115 us
  transfers between devices with their start and end apart: 3, of which 3 were waited for; matrix products, arithmetic and copies ran while one was open for 2% of the time, Pallas kernels for 0%

commit v1 on v0

v1 whole, which is shorter than its diff:
```python
import jax
import jax.numpy as jnp
from jax import lax
from jax.sharding import Mesh, PartitionSpec as P

AXES = ("yh", "zh", "zl", "core", "x", "yl")
SIZES = (4, 6, 2, 2, 4, 2)
DP = AXES[:4]
EP = AXES[4:]
FAR = ("yh", "zh")
N_FAR = 24
N_EP = 8
SWAP = [(0, 1), (1, 0)]


def route_block(routes, chances, capacity):
    matches = routes == 0
    chosen = jnp.any(matches, axis=1).astype(jnp.int32)
    weight = jnp.sum(jnp.where(matches, chances, jnp.zeros_like(chances)), axis=1)
    earlier = jnp.cumsum(chosen) - chosen
    retained = (chosen > 0) & (earlier < capacity)
    placement = (
        (earlier[None, :] == jnp.arange(capacity, dtype=jnp.int32)[:, None]) & retained[None, :]
    ).astype(jnp.float32)
    return (placement, weight)


def spread(value, axes, n):
    copies = jnp.broadcast_to(value[None], (n,) + value.shape)
    return lax.all_to_all(copies, axes, 0, 0, tiled=True)


def local(grad_out, expert_ids, route_probs, saved_inputs, w_gate, w_up, w_down):
    capacity = grad_out.shape[0] // 8
    units, width = w_gate.shape
    slots = N_FAR * capacity
    share = 4 * units // N_EP

    own = jnp.stack([w_gate, w_up, w_down])
    near = lax.ppermute(own, "core", SWAP)
    across = lax.ppermute(own, "zl", SWAP)
    diagonal = lax.ppermute(across, "core", SWAP)
    weights = jnp.stack([own, near, across, diagonal], axis=1).reshape(3, 4 * units, width)

    placement, weight = route_block(expert_ids, route_probs, capacity)
    residual = grad_out.astype(jnp.float32)
    weighted = weight[:, None] * residual
    outgoing = jnp.dot(placement, weighted, precision=lax.Precision.HIGHEST).astype(jnp.bfloat16)
    gathered = spread(spread(outgoing, "zh", 6).reshape(6 * capacity, width), "yh", 4).reshape(slots, width)

    member = lax.axis_index("zl") * 2 + lax.axis_index("core")
    saved = lax.dynamic_index_in_dim(
        saved_inputs.reshape(N_FAR, 4, capacity, width), member, axis=1, keepdims=False
    ).reshape(slots, width)

    dims = (((1,), (1,)), ((), ()))
    gate_part = lax.dot_general(weights[0], saved, dims, preferred_element_type=jnp.float32)
    up_part = lax.dot_general(weights[1], saved, dims, preferred_element_type=jnp.float32)
    hid_part = lax.dot_general(weights[2], gathered, dims, preferred_element_type=jnp.float32)
    parts = jnp.stack(
        [p.astype(jnp.bfloat16).reshape(N_EP, share, slots) for p in (gate_part, up_part, hid_part)], axis=1
    )
    parts = lax.all_to_all(parts, EP, 0, 0, tiled=True)
    gate_pre, up_pre, hid_grad = jnp.sum(parts.astype(jnp.float32), axis=0)

    sigmoid_gate = jax.nn.sigmoid(gate_pre)
    activated = gate_pre * sigmoid_gate
    hidden = (activated * up_pre).astype(jnp.bfloat16)
    gate_slope = sigmoid_gate + gate_pre * sigmoid_gate * (1.0 - sigmoid_gate)
    gate_grad = (hid_grad * up_pre * gate_slope).astype(jnp.bfloat16)
    up_grad = (hid_grad * activated).astype(jnp.bfloat16)
    whole = spread(jnp.stack([gate_grad, up_grad, hidden]), EP, N_EP)
    gate_grad, up_grad, hidden = [whole[:, k].reshape(4 * units, slots) for k in range(3)]

    grads = jnp.stack(
        [
            jnp.dot(gate_grad, saved, preferred_element_type=jnp.float32),
            jnp.dot(up_grad, saved, preferred_element_type=jnp.float32),
            jnp.dot(hidden, gathered, preferred_element_type=jnp.float32),
        ]
    ).reshape(3, 4, units, width)
    from_near = lax.ppermute(grads[:, 1::2].astype(jnp.bfloat16), "core", SWAP)

    dims = (((0,), (0,)), ((), ()))
    slot_part = lax.dot_general(gate_grad, weights[0], dims, preferred_element_type=jnp.float32) + lax.dot_general(
        up_grad, weights[1], dims, preferred_element_type=jnp.float32
    )
    half = grads[:, 0::2] + from_near.astype(jnp.float32)
    from_across = lax.ppermute(half[:, 1].astype(jnp.bfloat16), "zl", SWAP)

    slot_part = slot_part.astype(jnp.bfloat16).reshape(4, 6 * capacity, width)
    slot_part = jnp.sum(lax.all_to_all(slot_part, "yh", 0, 0, tiled=True).astype(jnp.float32), axis=0)
    slot_part = slot_part.astype(jnp.bfloat16).reshape(6, capacity, width)
    own_slots = jnp.sum(lax.all_to_all(slot_part, "zh", 0, 0, tiled=True).astype(jnp.float32), axis=0)
    own_slots = own_slots.astype(jnp.bfloat16)

    grad_gate, grad_up, grad_down = half[:, 0] + from_across.astype(jnp.float32)
    routed = jnp.dot(placement.T, own_slots.astype(jnp.float32), precision=lax.Precision.HIGHEST)
    grad_in = (residual + routed).astype(jnp.bfloat16)
    return (grad_in, grad_gate, grad_up, grad_down)


def solution(mesh):
    fine = Mesh(mesh.devices.reshape(SIZES), AXES)
    in_specs = (P(DP, EP), P(DP, None), P(DP, None), P(None, EP), P(DP, EP), P(DP, EP), P(DP, EP))
    return jax.shard_map(local, mesh=fine, in_specs=in_specs, out_specs=(P(DP, EP),) * 4, check_vma=False)
```

time: 490 us -> 173 us (0.35)
  the two profiles are of different devices: /device:TPU:4 before, /device:TPU:16 now
where the time goes in v1:
time: 173 us; the launch traced here: 172 us
  waiting for transfers between devices  54.7 us (32%)
  starting transfers between devices  45.3 us (26%)
  blocking collectives  36.6 us (21%)
  other arithmetic  16.3 us (9%)
  matrix products  9.78 us (6%)
  local copies, waits for them, and re-layouts  8.77 us (5%)
    all_to_all x2, starting transfers between devices, spread(): return lax.all_to_all(copies, axes, 0, 0, tiled=True)  21.6 us
    all_to_all x2, waiting for transfers between devices, spread(): return lax.all_to_all(copies, axes, 0, 0, tiled=True)  20.2 us
    all_to_all x1, blocking collectives, local(): parts = lax.all_to_all(parts, EP, 0, 0, tiled=True)  19.5 us
    all_to_all x1, blocking collectives, spread(): return lax.all_to_all(copies, axes, 0, 0, tiled=True)  17.1 us
    all_to_all x1, waiting for transfers between devices, local(): lax.all_to_all(slot_part, 'yh', 0, 0, tiled=True).astype(jnp.float32)  12.9 us
    ppermute x1, waiting for transfers between devices, local(): across = lax.ppermute(own, 'zl', SWAP)  10.9 us
    ppermute x1, waiting for transfers between devices, local(): from_across = lax.ppermute(half[:, 1].astype(jnp.bfloat16), 'zl', SWAP)  6.57 us
    all_to_all x1, starting transfers between devices, local(): lax.all_to_all(slot_part, 'zh', 0, 0, tiled=True).astype(jnp.float32)  5.89 us
  transfers between devices with their start and end apart: 9, of which 6 were waited for; matrix products, arithmetic and copies ran while one was open for 12% of the time, Pallas kernels for 0%

profile of v1, /device:TPU:16, one launch (start us, length us, event | category | flops | bytes accessed | tf_op | source)
XLA Modules:
  0.0 172.3 jit_solution(14166422889347636121)
XLA Ops:
  0.6 2.3 %fusion.12 = (bf16[3,1,112,768]{3,2,0,1:T(8,128)(2,1)}, bf16[3,112,768]{2,1,0:T(8,128)(2,1)}) fusion(bf16[1,112,768]{2,1,0:T(8,128)(2,1)} %bitcast.98, bf16[1,112,768]{2,1,0:T(8,128)(2,1)} %bitcast.99, bf16[1,112,768]{2,1,0:T(8,128)(2,1)} %bitcast.100), kind=kLoop, calls=%fused_computation.44 | loop fusion | flops 516096 | bytes 1548288 | tf_op jit(solution)/shard_map/stack | solution.py:43
  2.9 1.9 %collective-permute-start = (bf16[3,112,768]{2,1,0:T(8,128)(2,1)}, bf16[3,112,768]{2,1,0:T(8,128)(2,1)}, u32[]{:S(2)}, u32[]{:S(2)}) collective-permute-start(bf16[3,112,768]{2,1,0:T(8,128)(2,1)} %get-tuple-element.16), channel_id=1, source_target_pairs={{0,8},{8,0},{1,9},{9,1},{2,10},{10,2},{3,11},{11,3},{4,12},{12,4},... | collective-permute-start | bytes 1548296 | tf_op jit(solution)/shard_map/ppermute | solution.py:40
  4.8 4.3 %collective-permute-start.1 = (bf16[3,112,768]{2,1,0:T(8,128)(2,1)}, bf16[3,112,768]{2,1,0:T(8,128)(2,1)}, u32[]{:S(2)}, u32[]{:S(2)}) collective-permute-start(bf16[3,112,768]{2,1,0:T(8,128)(2,1)} %get-tuple-element.16), channel_id=1, source_target_pairs={{0,16},{16,0},{1,17},{17,1},{2,18},{18,2},{3,19},{19,3},{4,20},{20... | collective-permute-start | bytes 1548296 | tf_op jit(solution)/shard_map/ppermute | solution.py:41
  11.0 10.9 %collective-permute-done.1 = bf16[3,112,768]{2,1,0:T(8,128)(2,1)} collective-permute-done((bf16[3,112,768]{2,1,0:T(8,128)(2,1)}, bf16[3,112,768]{2,1,0:T(8,128)(2,1)}, u32[]{:S(2)}, u32[]{:S(2)}) %collective-permute-start.1) | collective-permute-done | bytes 516128 | tf_op jit(solution)/shard_map/ppermute | solution.py:41
  21.8 1.9 %collective-permute-start.2 = (bf16[3,112,768]{2,1,0:T(8,128)(2,1)}, bf16[3,112,768]{2,1,0:T(8,128)(2,1)}, u32[]{:S(2)}, u32[]{:S(2)}) collective-permute-start(bf16[3,112,768]{2,1,0:T(8,128)(2,1)} %collective-permute-done.1), channel_id=1, source_target_pairs={{0,8},{8,0},{1,9},{9,1},{2,10},{10,2},{3,11},{11,3},{4,12},{12,4},... | collective-permute-start | bytes 1548296 | tf_op jit(solution)/shard_map/ppermute | solution.py:42
  25.7 14.2 %all-to-all-start = ((bf16[6,16,768]{2,1,0:T(8,128)(2,1)}), bf16[6,16,768]{2,1,0:T(8,128)(2,1)S(1)}, u32[]{:S(2)}, u32[]{:S(2)}) async-start(bf16[6,16,768]{2,1,0:T(8,128)(2,1)} %broadcast_in_dim.11), calls=%async_computation | async-start | bytes 294912 | tf_op jit(solution)/shard_map/all_to_all | solution.py:30
  40.0 12.2 %all-to-all-done = bf16[6,16,768]{2,1,0:T(8,128)(2,1)S(1)} async-done(((bf16[6,16,768]{2,1,0:T(8,128)(2,1)}), bf16[6,16,768]{2,1,0:T(8,128)(2,1)S(1)}, u32[]{:S(2)}, u32[]{:S(2)}) %all-to-all-start) | async-done | bytes 147488 | tf_op jit(solution)/shard_map/all_to_all | solution.py:30
  53.1 7.4 %all-to-all-start.1 = ((bf16[4,96,768]{2,1,0:T(8,128)(2,1)}), bf16[4,96,768]{2,1,0:T(8,128)(2,1)S(1)}, u32[]{:S(2)}, u32[]{:S(2)}) async-start(bf16[4,96,768]{2,1,0:T(8,128)(2,1)} %broadcast_in_dim.13), calls=%async_computation.1 | async-start | bytes 1179648 | tf_op jit(solution)/shard_map/all_to_all | solution.py:30
  60.5 1.8 %pad_maximum_fusion.1 = bf16[3,4,112,768]{3,2,0,1:T(8,128)(2,1)S(1)} fusion(bf16[3,1,112,768]{3,2,0,1:T(8,128)(2,1)} %bitcast.7, bf16[3,1,112,768]{3,2,0,1:T(8,128)(2,1)} %bitcast.6, bf16[3,1,112,768]{3,2,0,1:T(8,128)(2,1)} %bitcast.5, bf16[3,1,112,768]{3,2,0,1:T(8,128)(2,1)} %get-tuple-element.15), kind=kLoop, calls=%fused_computation.1 | loop fusion | flops 3096576 | bytes 4128768 | tf_op jit(solution)/shard_map/stack | solution.py:43
  66.7 8.0 %all-to-all-done.1 = bf16[4,96,768]{2,1,0:T(8,128)(2,1)S(1)} async-done(((bf16[4,96,768]{2,1,0:T(8,128)(2,1)}), bf16[4,96,768]{2,1,0:T(8,128)(2,1)S(1)}, u32[]{:S(2)}, u32[]{:S(2)}) %all-to-all-start.1) | async-done | bytes 589856 | tf_op jit(solution)/shard_map/all_to_all | solution.py:30
  74.7 1.6 convolution_convert_fusion
  77.5 19.5 %all_to_all.30 = bf16[8,3,56,384]{3,2,1,0:T(8,128)(2,1)S(1)} all-to-all(bf16[8,3,56,384]{3,2,1,0:T(8,128)(2,1)S(1)} %pad_maximum_fusion.2), channel_id=1, replica_groups=mesh['yh'=4,'zh'=6,'zl'=2,'core'=2,'x'=4,'yl'=2] {'x','yl'}, dimensions={0} | all-to-all | bytes 2064384 | tf_op jit(solution)/shard_map/all_to_all | solution.py:63
  97.4 17.1 %all_to_all.31 = bf16[8,3,56,384]{3,2,1,0:T(8,128)(2,1)S(1)} all-to-all(bf16[8,3,56,384]{3,2,1,0:T(8,128)(2,1)S(1)} %broadcast_in_dim.14), channel_id=1, replica_groups=mesh['yh'=4,'zh'=6,'zl'=2,'core'=2,'x'=4,'yl'=2] {'x','yl'}, dimensions={0} | all-to-all | bytes 2064384 | tf_op jit(solution)/shard_map/all_to_all | solution.py:30
  118.9 1.9 %collective-permute-start.3 = (bf16[3,2,112,768]{3,2,1,0:T(8,128)(2,1)}, bf16[3,2,112,768]{3,2,1,0:T(8,128)(2,1)}, u32[]{:S(2)}, u32[]{:S(2)}) collective-permute-start(bf16[3,2,112,768]{3,2,1,0:T(8,128)(2,1)} %slice.44), channel_id=1, source_target_pairs={{0,8},{8,0},{1,9},{9,1},{2,10},{10,2},{3,11},{11,3},{4,12},{12,4},... | collective-permute-start | bytes 3096584 | tf_op jit(solution)/shard_map/ppermute | solution.py:82
  120.9 1.3 fusion
  122.2 4.2 %all-to-all-start.4 = ((bf16[4,96,768]{2,1,0:T(8,128)(2,1)}), bf16[4,96,768]{2,1,0:T(8,128)(2,1)S(1)}, u32[]{:S(2)}, u32[]{:S(2)}) async-start(bf16[4,96,768]{2,1,0:T(8,128)(2,1)} %bitcast.23), calls=%async_computation.4 | async-start | bytes 1179648 | tf_op jit(solution)/shard_map/all_to_all | solution.py:92
  126.4 4.3 %pad_maximum_fusion = f32[3,4,112,768]{3,2,1,0:T(8,128)} fusion(f32[1,4,112,768]{3,2,1,0:T(8,128)} %copy-done.3, f32[1,4,112,768]{3,2,1,0:T(8,128)} %copy-done.2, f32[1,4,112,768]{3,2,1,0:T(8,128)} %copy-done.1), kind=kLoop, calls=%fused_computation | loop fusion | flops 2064384 | bytes 8257536 | tf_op jit(solution)/shard_map/stack | solution.py:75
  130.7 12.9 %all-to-all-done.4 = bf16[4,96,768]{2,1,0:T(8,128)(2,1)S(1)} async-done(((bf16[4,96,768]{2,1,0:T(8,128)(2,1)}), bf16[4,96,768]{2,1,0:T(8,128)(2,1)S(1)}, u32[]{:S(2)}, u32[]{:S(2)}) %all-to-all-start.4) | async-done | bytes 589856 | tf_op jit(solution)/shard_map/all_to_all | solution.py:92
  144.4 5.9 %all-to-all-start.5 = ((bf16[6,16,768]{2,1,0:T(8,128)(2,1)}), bf16[6,16,768]{2,1,0:T(8,128)(2,1)S(1)}, u32[]{:S(2)}, u32[]{:S(2)}) async-start(bf16[6,16,768]{2,1,0:T(8,128)(2,1)} %bitcast.24), calls=%async_computation.5 | async-start | bytes 294912 | tf_op jit(solution)/shard_map/all_to_all | solution.py:94
  150.3 2.2 %convert_add_fusion = f32[3,2,112,768]{3,2,1,0:T(8,128)S(1)} fusion(bf16[3,2,112,768]{3,2,1,0:T(8,128)(2,1)} %collective-permute-done.3, f32[3,4,112,768]{3,2,1,0:T(8,128)} %pad_maximum_fusion), kind=kLoop, calls=%fused_computation.2 | loop fusion | flops 1032192 | bytes 5160960 | tf_op jit(solution)/shard_map/add | solution.py:88
  152.5 1.3 copy-done.4
  154.7 3.6 %collective-permute-start.4 = (bf16[3,112,768]{2,1,0:T(8,128)(2,1)}, bf16[3,112,768]{2,1,0:T(8,128)(2,1)S(1)}, u32[]{:S(2)}, u32[]{:S(2)}) collective-permute-start(bf16[3,112,768]{2,1,0:T(8,128)(2,1)} %fusion.3), channel_id=1, source_target_pairs={{0,16},{16,0},{1,17},{17,1},{2,18},{18,2},{3,19},{19,3},{4,20},{20... | collective-permute-start | bytes 1548296 | tf_op jit(solution)/shard_map/ppermute | solution.py:89
  158.3 4.2 %all-to-all-done.5 = bf16[6,16,768]{2,1,0:T(8,128)(2,1)S(1)} async-done(((bf16[6,16,768]{2,1,0:T(8,128)(2,1)}), bf16[6,16,768]{2,1,0:T(8,128)(2,1)S(1)}, u32[]{:S(2)}, u32[]{:S(2)}) %all-to-all-start.5) | async-done | bytes 147488 | tf_op jit(solution)/shard_map/all_to_all | solution.py:94
  163.4 6.6 %collective-permute-done.4 = bf16[3,112,768]{2,1,0:T(8,128)(2,1)S(1)} collective-permute-done((bf16[3,112,768]{2,1,0:T(8,128)(2,1)}, bf16[3,112,768]{2,1,0:T(8,128)(2,1)S(1)}, u32[]{:S(2)}, u32[]{:S(2)}) %collective-permute-start.4) | collective-permute-done | bytes 516128 | tf_op jit(solution)/shard_map/ppermute | solution.py:89
  (55 shorter events, 20.0 us)
Async XLA Ops:
  0.6 39.3 %copy-start = (bf16[1536,768]{1,0:T(8,128)(2,1)S(1)}, bf16[1536,768]{1,0:T(8,128)(2,1)}, u32[]{:S(2)}) copy-start(bf16[1536,768]{1,0:T(8,128)(2,1)} %param.10) | copy-start | bytes 7077892
  2.9 57.6 %collective-permute-start = (bf16[3,112,768]{2,1,0:T(8,128)(2,1)}, bf16[3,112,768]{2,1,0:T(8,128)(2,1)}, u32[]{:S(2)}, u32[]{:S(2)}) collective-permute-start(bf16[3,112,768]{2,1,0:T(8,128)(2,1)} %get-tuple-element.16), channel_id=1, source_target_pairs={{0,8},{8,0},{1,9},{9,1},{2,10},{10,2},{3,11},{11,3},{4,12},{12,4},... | collective-permute-start | bytes 1548296 | tf_op jit(solution)/shard_map/ppermute | solution.py:40
  4.8 17.0 %collective-permute-start.1 = (bf16[3,112,768]{2,1,0:T(8,128)(2,1)}, bf16[3,112,768]{2,1,0:T(8,128)(2,1)}, u32[]{:S(2)}, u32[]{:S(2)}) collective-permute-start(bf16[3,112,768]{2,1,0:T(8,128)(2,1)} %get-tuple-element.16), channel_id=1, source_target_pairs={{0,16},{16,0},{1,17},{17,1},{2,18},{18,2},{3,19},{19,3},{4,20},{20... | collective-permute-start | bytes 1548296 | tf_op jit(solution)/shard_map/ppermute | solution.py:41
  21.8 38.7 %collective-permute-start.2 = (bf16[3,112,768]{2,1,0:T(8,128)(2,1)}, bf16[3,112,768]{2,1,0:T(8,128)(2,1)}, u32[]{:S(2)}, u32[]{:S(2)}) collective-permute-start(bf16[3,112,768]{2,1,0:T(8,128)(2,1)} %collective-permute-done.1), channel_id=1, source_target_pairs={{0,8},{8,0},{1,9},{9,1},{2,10},{10,2},{3,11},{11,3},{4,12},{12,4},... | collective-permute-start | bytes 1548296 | tf_op jit(solution)/shard_map/ppermute | solution.py:42
  25.7 26.5 %all-to-all-start = ((bf16[6,16,768]{2,1,0:T(8,128)(2,1)}), bf16[6,16,768]{2,1,0:T(8,128)(2,1)S(1)}, u32[]{:S(2)}, u32[]{:S(2)}) async-start(bf16[6,16,768]{2,1,0:T(8,128)(2,1)} %broadcast_in_dim.11), calls=%async_computation | async-start | bytes 294912 | tf_op jit(solution)/shard_map/all_to_all | solution.py:30
  53.1 21.6 %all-to-all-start.1 = ((bf16[4,96,768]{2,1,0:T(8,128)(2,1)}), bf16[4,96,768]{2,1,0:T(8,128)(2,1)S(1)}, u32[]{:S(2)}, u32[]{:S(2)}) async-start(bf16[4,96,768]{2,1,0:T(8,128)(2,1)} %broadcast_in_dim.13), calls=%async_computation.1 | async-start | bytes 1179648 | tf_op jit(solution)/shard_map/all_to_all | solution.py:30
  63.3 0.9 copy-start.5
  63.3 2.1 %copy-start.7 = (bf16[1,4,112,768]{3,2,0,1:T(8,128)(2,1)}, bf16[1,4,112,768]{3,2,0,1:T(8,128)(2,1)S(1)}, u32[]{:S(2)}) copy-start(bf16[1,4,112,768]{3,2,0,1:T(8,128)(2,1)S(1)} %get-tuple-element.8) | copy-start | bytes 2064388
  97.4 17.2 %copy-start.8 = (bf16[1,4,112,768]{3,2,0,1:T(8,128)(2,1)S(1)}, bf16[1,4,112,768]{3,2,0,1:T(8,128)(2,1)}, u32[]{:S(2)}) copy-start(bf16[1,4,112,768]{3,2,0,1:T(8,128)(2,1)} %copy-done.7) | copy-start | bytes 2064388
  115.6 1.1 copy-start.1
  116.1 1.1 copy-start.2
  116.7 1.1 copy-start.3
  117.8 3.1 %copy-start.6 = (bf16[1,4,112,768]{3,2,0,1:T(8,128)(2,1)S(1)}, bf16[1,4,112,768]{3,2,0,1:T(8,128)(2,1)}, u32[]{:S(2)}) copy-start(bf16[1,4,112,768]{3,2,0,1:T(8,128)(2,1)} %copy-done.5) | copy-start | bytes 2064388
  118.9 31.4 %collective-permute-start.3 = (bf16[3,2,112,768]{3,2,1,0:T(8,128)(2,1)}, bf16[3,2,112,768]{3,2,1,0:T(8,128)(2,1)}, u32[]{:S(2)}, u32[]{:S(2)}) collective-permute-start(bf16[3,2,112,768]{3,2,1,0:T(8,128)(2,1)} %slice.44), channel_id=1, source_target_pairs={{0,8},{8,0},{1,9},{9,1},{2,10},{10,2},{3,11},{11,3},{4,12},{12,4},... | collective-permute-start | bytes 3096584 | tf_op jit(solution)/shard_map/ppermute | solution.py:82
  122.2 21.4 %all-to-all-start.4 = ((bf16[4,96,768]{2,1,0:T(8,128)(2,1)}), bf16[4,96,768]{2,1,0:T(8,128)(2,1)S(1)}, u32[]{:S(2)}, u32[]{:S(2)}) async-start(bf16[4,96,768]{2,1,0:T(8,128)(2,1)} %bitcast.23), calls=%async_computation.4 | async-start | bytes 1179648 | tf_op jit(solution)/shard_map/all_to_all | solution.py:92
  144.4 18.0 %all-to-all-start.5 = ((bf16[6,16,768]{2,1,0:T(8,128)(2,1)}), bf16[6,16,768]{2,1,0:T(8,128)(2,1)S(1)}, u32[]{:S(2)}, u32[]{:S(2)}) async-start(bf16[6,16,768]{2,1,0:T(8,128)(2,1)} %bitcast.24), calls=%async_computation.5 | async-start | bytes 294912 | tf_op jit(solution)/shard_map/all_to_all | solution.py:94
  150.3 12.2 %copy-start.9 = (bf16[128,768]{1,0:T(8,128)(2,1)S(1)}, bf16[128,768]{1,0:T(8,128)(2,1)}, u32[]{:S(2)}) copy-start(bf16[128,768]{1,0:T(8,128)(2,1)} %param.7) | copy-start | bytes 589828
  152.5 1.3 copy-start.4
  154.7 15.3 %collective-permute-start.4 = (bf16[3,112,768]{2,1,0:T(8,128)(2,1)}, bf16[3,112,768]{2,1,0:T(8,128)(2,1)S(1)}, u32[]{:S(2)}, u32[]{:S(2)}) collective-permute-start(bf16[3,112,768]{2,1,0:T(8,128)(2,1)} %fusion.3), channel_id=1, source_target_pairs={{0,16},{16,0},{1,17},{17,1},{2,18},{18,2},{3,19},{19,3},{4,20},{20... | collective-permute-start | bytes 1548296 | tf_op jit(solution)/shard_map/ppermute | solution.py:89

commit v2 on v1

v2 whole, which is shorter than its diff:
```python
import functools

import jax
import jax.numpy as jnp
from jax import lax
from jax.experimental import pallas as pl
from jax.experimental.pallas import tpu as pltpu
from jax.sharding import Mesh, PartitionSpec as P

AXES = ("yh", "zh", "zl", "core", "x", "yl")
SIZES = (4, 6, 2, 2, 4, 2)
DP = AXES[:4]
EP = AXES[4:]
N_YH = 4
N_ZH = 6
N_FAR = 24
N_EP = 8
SWAP = [(0, 1), (1, 0)]
BF16 = jnp.bfloat16
F32 = jnp.float32


VMEM = pltpu.VMEM
HBM = pltpu.HBM


def scratch_call(body, outs, scratch, flops, *args):
    moved = sum(a.size * a.dtype.itemsize for a in args)
    return pl.pallas_call(
        body,
        out_shape=outs,
        in_specs=[pl.BlockSpec(memory_space=VMEM)] * len(args),
        out_specs=[pl.BlockSpec(memory_space=VMEM)] * len(outs),
        scratch_shapes=[VMEM(scratch, BF16)],
        cost_estimate=pl.CostEstimate(flops=flops, bytes_accessed=moved, transcendentals=0),
        compiler_params=pltpu.CompilerParams(vmem_limit_bytes=24 * 1024 * 1024),
    )(*args)


def kernel_call(body, outs, flops, *args):
    moved = sum(a.size * a.dtype.itemsize for a in args)
    return pl.pallas_call(
        body,
        out_shape=outs,
        in_specs=[pl.BlockSpec(memory_space=VMEM)] * len(args),
        out_specs=[pl.BlockSpec(memory_space=VMEM)] * len(outs),
        cost_estimate=pl.CostEstimate(flops=flops, bytes_accessed=moved, transcendentals=0),
        compiler_params=pltpu.CompilerParams(vmem_limit_bytes=24 * 1024 * 1024),
    )(*args)


def array(*shape, dtype=BF16):
    return jax.ShapeDtypeStruct(shape, dtype)


def dot(a, b, dims):
    return lax.dot_general(a, b, (dims, ((), ())), preferred_element_type=F32)


ROWS = ((0,), (0,))
PLAIN = ((1,), (0,))
LANES = ((1,), (1,))


def route_kernel(
    grad_hbm, ids_hbm, probs_hbm, wg_hbm, wu_hbm, wd_hbm, copies_ref, placement_ref, own_ref, grad_ref, ids_ref, probs_ref, sems
):
    pairs = (
        (ids_hbm, ids_ref),
        (probs_hbm, probs_ref),
        (grad_hbm, grad_ref),
        (wg_hbm, own_ref.at[0]),
        (wu_hbm, own_ref.at[1]),
        (wd_hbm, own_ref.at[2]),
    )
    moves = [pltpu.make_async_copy(a, b, sems.at[i]) for i, (a, b) in enumerate(pairs)]
    for move in moves:
        move.start()
    tokens = grad_ref.shape[0]
    copies, capacity, _ = copies_ref.shape
    rows = lax.broadcasted_iota(jnp.int32, (tokens, tokens), 0)
    columns = lax.broadcasted_iota(jnp.int32, (tokens, tokens), 1)
    before = jnp.where(rows < columns, 1.0, 0.0).astype(BF16)
    slot = lax.broadcasted_iota(jnp.int32, (capacity, tokens), 0).astype(F32)
    moves[0].wait()
    moves[1].wait()
    matches = ids_ref[...] == 0
    chosen = jnp.max(jnp.where(matches, 1.0, 0.0), axis=0, keepdims=True)
    weight = jnp.sum(jnp.where(matches, probs_ref[...], 0.0), axis=0, keepdims=True)
    chosen = jnp.broadcast_to(chosen, (capacity, tokens))
    earlier = dot(chosen.astype(BF16), before, PLAIN)
    placement = jnp.where((earlier == slot) & (chosen > 0.5), 1.0, 0.0)
    placement_ref[...] = placement.astype(BF16)
    scale = jnp.sum(placement * weight, axis=1, keepdims=True)
    moves[2].wait()
    picked = dot(placement.astype(BF16), grad_ref[...], PLAIN)
    outgoing = (picked * scale).astype(BF16)
    for i in range(copies):
        copies_ref[i] = outgoing
    for move in moves[3:]:
        move.wait()


def copies_kernel(value_ref, copies_ref):
    for i in range(copies_ref.shape[0]):
        copies_ref[i] = value_ref[...]


def pre_kernel(own_ref, across_ref, near_ref, diagonal_ref, saved_ref, gathered_ref, parts_ref, w_ref):
    units = own_ref.shape[1]
    group = 4 * units
    for k in range(3):
        for i, ref in enumerate((own_ref, across_ref, near_ref, diagonal_ref)):
            w_ref[k * group + i * units : k * group + (i + 1) * units] = ref[k]
    parts_ref[:, : 2 * group] = dot(saved_ref[...], w_ref[: 2 * group], LANES).astype(BF16)
    parts_ref[:, 2 * group :] = dot(gathered_ref[...], w_ref[2 * group :], LANES).astype(BF16)


def activation_kernel(parts_ref, copies_ref):
    sources, _, wide = parts_ref.shape
    group = wide // 3
    total = parts_ref[0].astype(F32)
    for i in range(1, sources):
        total += parts_ref[i].astype(F32)
    gate_pre, up_pre, hid_grad = (total[:, k * group : (k + 1) * group] for k in range(3))
    sigmoid_gate = jax.nn.sigmoid(gate_pre)
    activated = gate_pre * sigmoid_gate
    gate_slope = sigmoid_gate + gate_pre * sigmoid_gate * (1.0 - sigmoid_gate)
    gate_grad = hid_grad * up_pre * gate_slope
    act = jnp.concatenate([gate_grad, hid_grad * activated, activated * up_pre], axis=1).astype(BF16)
    for i in range(sources):
        copies_ref[i] = act


def weight_grads(act_ref, saved_ref, gathered_ref, k, half):
    group = act_ref.shape[1] // 3
    start = k * group + half * group // 2
    low = start // 128 * 128
    high = min((start + group // 2 + 127) // 128 * 128, 3 * group)
    part = dot(act_ref[:, low:high], (gathered_ref if k == 2 else saved_ref)[...], ROWS)
    return part[start - low : start - low + group // 2]


def slot_kernel(
    act_ref, saved_ref, gathered_ref, own, across, near, diagonal, slot_hbm, sent_hbm, w_ref, slot_ref, sent_ref, in_sems, out_sems
):
    units = own.shape[1]
    group = 4 * units
    fetches = []
    for k in range(2):
        for i, piece in enumerate((own, across, near, diagonal)):
            place = w_ref.at[pl.ds(k * group + i * units, units)]
            fetches.append(pltpu.make_async_copy(piece.at[k], place, in_sems.at[4 * k + i]))
    for fetch in fetches:
        fetch.start()
    stores = []
    for k in range(3):
        sent_ref[k] = weight_grads(act_ref, saved_ref, gathered_ref, k, 1).astype(BF16)
        stores.append(pltpu.make_async_copy(sent_ref.at[k], sent_hbm.at[k], out_sems.at[k]))
        stores[k].start()
    for fetch in fetches:
        fetch.wait()
    slot_ref[...] = dot(act_ref[:, : 2 * group], w_ref[...], PLAIN).astype(BF16)
    stores.append(pltpu.make_async_copy(slot_ref, slot_hbm, out_sems.at[3]))
    stores[3].start()
    for store in stores:
        store.wait()


def kept_kernel(act_ref, saved_ref, gathered_ref, near_ref, own_ref, sent_ref):
    units = own_ref.shape[1]
    for k in range(3):
        part = weight_grads(act_ref, saved_ref, gathered_ref, k, 0)
        own_ref[k] = part[:units] + near_ref[k, :units].astype(F32)
        sent_ref[k] = (part[units:] + near_ref[k, units:].astype(F32)).astype(BF16)


def sum_kernel(parts_ref, total_ref):
    total = parts_ref[0].astype(F32)
    for i in range(1, parts_ref.shape[0]):
        total += parts_ref[i].astype(F32)
    total_ref[...] = total.astype(BF16)


def result_kernel(parts_ref, placement_ref, grad_ref, result_ref):
    total = parts_ref[0].astype(F32)
    for i in range(1, parts_ref.shape[0]):
        total += parts_ref[i].astype(F32)
    routed = dot(placement_ref[...], total.astype(BF16), ROWS)
    result_ref[...] = (grad_ref[...].astype(F32) + routed).astype(BF16)


def local(grad_out, expert_ids, route_probs, saved_inputs, w_gate, w_up, w_down):
    tokens, width = grad_out.shape
    capacity = tokens // 8
    units = w_gate.shape[0]
    slots = N_FAR * capacity
    group = 4 * units

    copies, placement, own = pl.pallas_call(
        route_kernel,
        out_shape=[array(N_ZH, capacity, width), array(capacity, tokens), HBM((3, units, width), BF16)],
        in_specs=[pl.BlockSpec(memory_space=pl.ANY)] * 6,
        out_specs=[pl.BlockSpec(memory_space=VMEM)] * 3,
        scratch_shapes=[
            VMEM((tokens, width), BF16),
            VMEM(expert_ids.shape[::-1], jnp.int32),
            VMEM(route_probs.shape[::-1], F32),
            pltpu.SemaphoreType.DMA((6,)),
        ],
    )(grad_out, expert_ids.T, route_probs.T, w_gate, w_up, w_down)

    copies = lax.all_to_all(copies, "zh", 0, 0, tiled=True).reshape(N_ZH * capacity, width)
    copies, own = lax.optimization_barrier((copies, own))
    near = lax.ppermute(own, "core", SWAP)
    across = lax.ppermute(own, "zl", SWAP)
    (copies,) = kernel_call(copies_kernel, [HBM((N_YH, N_ZH * capacity, width), BF16)], 0, copies)
    diagonal = lax.ppermute(across, "core", SWAP)
    gathered = lax.all_to_all(copies, "yh", 0, 0, tiled=True).reshape(slots, width)

    member = lax.axis_index("zl") * 2 + lax.axis_index("core")
    saved = lax.dynamic_index_in_dim(
        saved_inputs.reshape(N_FAR, 4, capacity, width), member, axis=1, keepdims=False
    ).reshape(slots, width)

    pieces = (own, across, near, diagonal)
    (parts,) = scratch_call(
        pre_kernel, [array(slots, 3 * group)], (3 * group, width), 6 * slots * group * width, *pieces, saved, gathered
    )
    parts = lax.all_to_all(parts.reshape(N_EP, slots // N_EP, 3 * group), EP, 0, 0, tiled=True)
    (copies,) = kernel_call(activation_kernel, [array(*parts.shape)], 20 * parts.size, parts)
    act = lax.all_to_all(copies, EP, 0, 0, tiled=True)
    act = act.reshape(slots, 3 * group)

    slot_part, sent = pl.pallas_call(
        slot_kernel,
        out_shape=[HBM((slots, width), BF16), HBM((3, 2 * units, width), BF16)],
        in_specs=[pl.BlockSpec(memory_space=VMEM)] * 3 + [pl.BlockSpec(memory_space=pl.ANY)] * 4,
        out_specs=[pl.BlockSpec(memory_space=pl.ANY)] * 2,
        scratch_shapes=[
            VMEM((2 * group, width), BF16),
            VMEM((slots, width), BF16),
            VMEM((3, 2 * units, width), BF16),
            pltpu.SemaphoreType.DMA((8,)),
            pltpu.SemaphoreType.DMA((4,)),
        ],
        cost_estimate=pl.CostEstimate(flops=7 * slots * group * width, bytes_accessed=6000000, transcendentals=0),
        compiler_params=pltpu.CompilerParams(vmem_limit_bytes=24 * 1024 * 1024),
    )(act, saved, gathered, *pieces)

    from_near = lax.ppermute(sent, "core", SWAP)
    slot_part = lax.all_to_all(slot_part.reshape(N_YH, N_ZH * capacity, width), "yh", 0, 0, tiled=True)
    kept, sent = kernel_call(
        kept_kernel,
        [HBM((3, units, width), F32), HBM((3, units, width), BF16)],
        6 * slots * group * width,
        act,
        saved,
        gathered,
        from_near,
    )
    from_across = lax.ppermute(sent, "zl", SWAP)
    (slot_part,) = kernel_call(sum_kernel, [HBM((N_ZH * capacity, width), BF16)], slot_part.size, slot_part)
    slot_part, from_across = lax.optimization_barrier((slot_part, from_across))
    slot_part = lax.all_to_all(slot_part.reshape(N_ZH, capacity, width), "zh", 0, 0, tiled=True)
    (grad_in,) = kernel_call(result_kernel, [array(tokens, width)], tokens * width * 32, slot_part, placement, grad_out)

    grad_gate, grad_up, grad_down = [kept[k] + from_across[k].astype(F32) for k in range(3)]
    return (grad_in, grad_gate, grad_up, grad_down)


def solution(mesh):
    fine = Mesh(mesh.devices.reshape(SIZES), AXES)
    in_specs = (P(DP, EP), P(DP, None), P(DP, None), P(None, EP), P(DP, EP), P(DP, EP), P(DP, EP))
    return jax.shard_map(local, mesh=fine, in_specs=in_specs, out_specs=(P(DP, EP),) * 4, check_vma=False)
```

time: 173 us -> 147 us (0.85)
  waiting for transfers between devices: 54.7 us -> 28.7 us
  blocking collectives: 36.6 us -> 57.8 us
  Pallas kernels: 0 us -> 16.5 us
  other arithmetic: 16.3 us -> 2.22 us
  matrix products: 9.78 us -> 0 us
  starting transfers between devices: 45.3 us -> 37.4 us
  local copies, waits for them, and re-layouts: 8.77 us -> 2.21 us
    all_to_all x2 -> x3, blocking collectives: 36.6 us -> 57.8 us  [the longest x1 26.6 us: local(): lax.all_to_all(copies, 'zh', 0, 0, tiled=True)]
    pallas_call x0 -> x8, Pallas kernels: none -> 16.5 us  [the longest x5 7.07 us: kernel_call(): pl.pallas_call(body, out_shape=outs, in_specs=[pl.BlockSpec(memory_space=...]
    all_to_all x4 -> x3, waiting for transfers between devices: 37.3 us -> 26 us  [the longest x1 9.17 us: local(): lax.all_to_all(slot_part.reshape(N_ZH, capacity, width), 'zh', 0, 0, tile...]
    ppermute x1, waiting for transfers between devices: 10.9 us -> 0.01 us  [local(): across = lax.ppermute(own, 'zl', SWAP)]
    another operation x8 -> x0, other arithmetic: 10.4 us -> none  [the longest x1 4.35 us: local(): jnp.stack([jnp.dot(gate_grad, saved, preferred_element_type=jnp.float32),...]
    dot_general x10 -> x0, matrix products: 9.78 us -> none  [the longest x1 1.64 us: local(): lax.dot_general(weights[2], gathered, dims, preferred_element_type=jnp.fl...]
    all_to_all x4 -> x3, starting transfers between devices: 31.7 us -> 23.5 us  [the longest x1 10.9 us: local(): lax.all_to_all(slot_part.reshape(N_ZH, capacity, width), 'zh', 0, 0, tile...]
    ppermute x2, waiting for transfers between devices: 6.58 us -> 2.68 us  [the longest x1 2.68 us: local(): from_across = lax.ppermute(sent, 'zl', SWAP)]
  transfers between devices with their start and end apart: 9 -> 8, of which waited for: 6 -> 4; matrix products, arithmetic and copies ran while one was open for 12% -> 2% of each run, Pallas kernels for 0% -> 4%
where the time goes in v2:
time: 147 us; the launch traced here: 146 us
  blocking collectives  57.8 us (39%)
  starting transfers between devices  37.4 us (25%)
  waiting for transfers between devices  28.7 us (20%)
  Pallas kernels  16.5 us (11%)
  other arithmetic  2.22 us (2%)
  local copies, waits for them, and re-layouts  2.21 us (2%)
    all_to_all x1, blocking collectives, local(): lax.all_to_all(copies, 'zh', 0, 0, tiled=True)  26.6 us
    all_to_all x1, blocking collectives, local(): lax.all_to_all(parts.reshape(N_EP, slots // N_EP, 3 * group), EP, 0, 0, t...  16.8 us
    all_to_all x1, blocking collectives, local(): act = lax.all_to_all(copies, EP, 0, 0, tiled=True)  14.4 us
    all_to_all x1, starting transfers between devices, local(): lax.all_to_all(slot_part.reshape(N_ZH, capacity, width), 'zh', 0, 0, tile...  10.9 us
    all_to_all x1, waiting for transfers between devices, local(): lax.all_to_all(slot_part.reshape(N_ZH, capacity, width), 'zh', 0, 0, tile...  9.17 us
    all_to_all x1, waiting for transfers between devices, local(): lax.all_to_all(copies, 'yh', 0, 0, tiled=True).reshape(slots, width)  8.87 us
    all_to_all x1, waiting for transfers between devices, local(): lax.all_to_all(slot_part.reshape(N_YH, N_ZH * capacity, width), 'yh', 0,...  7.99 us
    all_to_all x1, starting transfers between devices, local(): lax.all_to_all(copies, 'yh', 0, 0, tiled=True).reshape(slots, width)  7.43 us
  transfers between devices with their start and end apart: 8, of which 4 were waited for; matrix products, arithmetic and copies ran while one was open for 2% of the time, Pallas kernels for 4%

profile of v2, /device:TPU:16, one launch (start us, length us, event | category | flops | bytes accessed | tf_op | source)
XLA Modules:
  0.0 145.7 jit_solution(5547556375712061489)
XLA Ops:
  0.6 2.3 %shard_map.102 = (bf16[6,16,768]{2,1,0:T(8,128)(2,1)}, bf16[16,128]{1,0:T(8,128)(2,1)}, bf16[3,112,768]{2,1,0:T(8,128)(2,1)}) custom-call(bf16[128,768]{1,0:T(8,128)(2,1)} %grad_ref.1, s32[4,128]{1,0:T(4,128)} %bitcast.31, f32[4,128]{1,0:T(4,128)} %bitcast.32, bf16[112,768]{1,0:T(8,128)(2,1)} %wg_hbm.1, bf16[112,768]{1,0:T(8,128)(2,1)} %wu_hbm.1, ...), custom_call_target="tpu_custom_call" | custom-call | tf_op jit(solution)/shard_map/pallas_call | solution.py:200
  2.9 26.6 %all_to_all.30 = bf16[6,16,768]{2,1,0:T(8,128)(2,1)S(1)} all-to-all(bf16[6,16,768]{2,1,0:T(8,128)(2,1)} %get-tuple-element.15), channel_id=1, replica_groups=mesh['yh'=4,'zh'=6,'zl'=2,'core'=2,'x'=4,'yl'=2] {'zh'}, dimensions={0} | all-to-all | bytes 294912 | tf_op jit(solution)/shard_map/all_to_all | solution.py:213
  29.5 3.6 %collective-permute-start = (bf16[3,112,768]{2,1,0:T(8,128)(2,1)}, bf16[3,112,768]{2,1,0:T(8,128)(2,1)}, u32[]{:S(2)}, u32[]{:S(2)}) collective-permute-start(bf16[3,112,768]{2,1,0:T(8,128)(2,1)} %get-tuple-element.17.own_ref.own), channel_id=1, source_target_pairs={{0,16},{16,0},{1,17},{17,1},{2,18},{18,2},{3,19},{19,3},{4,20},{20... | collective-permute-start | bytes 1548296 | tf_op jit(solution)/shard_map/ppermute | solution.py:216
  34.0 7.4 %all-to-all-start.1 = ((bf16[4,96,768]{2,1,0:T(8,128)(2,1)}), bf16[4,96,768]{2,1,0:T(8,128)(2,1)S(1)}, u32[]{:S(2)}, u32[]{:S(2)}) async-start(bf16[4,96,768]{2,1,0:T(8,128)(2,1)} %shard_map.103), calls=%async_computation.1 | async-start | bytes 1179648 | tf_op jit(solution)/shard_map/all_to_all | solution.py:219
  41.4 1.9 %collective-permute-start.1 = (bf16[3,112,768]{2,1,0:T(8,128)(2,1)}, bf16[3,112,768]{2,1,0:T(8,128)(2,1)}, u32[]{:S(2)}, u32[]{:S(2)}) collective-permute-start(bf16[3,112,768]{2,1,0:T(8,128)(2,1)} %get-tuple-element.17.own_ref.own), channel_id=1, source_target_pairs={{0,8},{8,0},{1,9},{9,1},{2,10},{10,2},{3,11},{11,3},{4,12},{12,4},... | collective-permute-start | bytes 1548296 | tf_op jit(solution)/shard_map/ppermute | solution.py:215
  43.3 2.4 %collective-permute-start.2 = (bf16[3,112,768]{2,1,0:T(8,128)(2,1)}, bf16[3,112,768]{2,1,0:T(8,128)(2,1)}, u32[]{:S(2)}, u32[]{:S(2)}) collective-permute-start(bf16[3,112,768]{2,1,0:T(8,128)(2,1)} %collective-permute-done.across_ref.across), channel_id=1, source_target_pairs={{0,8},{8,0},{1,9},{9,1},{2,10},{10,2},{3,11},{11,3},{4,12},{12,4},... | collective-permute-start | bytes 1548296 | tf_op jit(solution)/shard_map/ppermute | solution.py:218
  45.8 8.9 %all-to-all-done.1 = bf16[4,96,768]{2,1,0:T(8,128)(2,1)S(1)} async-done(((bf16[4,96,768]{2,1,0:T(8,128)(2,1)}), bf16[4,96,768]{2,1,0:T(8,128)(2,1)S(1)}, u32[]{:S(2)}, u32[]{:S(2)}) %all-to-all-start.1) | async-done | bytes 589856 | tf_op jit(solution)/shard_map/all_to_all | solution.py:219
  54.7 2.8 %shard_map.104 = bf16[384,1344]{1,0:T(8,128)(2,1)S(1)} custom-call(bf16[3,112,768]{2,1,0:T(8,128)(2,1)} %get-tuple-element.17.own_ref.own, bf16[3,112,768]{2,1,0:T(8,128)(2,1)} %collective-permute-done.across_ref.across, bf16[3,112,768]{2,1,0:T(8,128)(2,1)} %collective-permute-done.1.near_ref.near, ...), custom_call_target="tpu_custom_call" | custom-call | flops 792723456 | bytes 3244032 | tf_op jit(solution)/shard_map/pallas_call | solution.py:29
  57.6 16.8 %all_to_all.31.parts_ref = bf16[8,48,1344]{2,1,0:T(8,128)(2,1)S(1)} all-to-all(bf16[8,48,1344]{2,1,0:T(8,128)(2,1)S(1)} %bitcast.27), channel_id=1, replica_groups=mesh['yh'=4,'zh'=6,'zl'=2,'core'=2,'x'=4,'yl'=2] {'x','yl'}, dimensions={0} | all-to-all | bytes 2064384 | tf_op jit(solution)/shard_map/all_to_all | solution.py:230
  74.7 14.4 %all_to_all.32 = bf16[8,48,1344]{2,1,0:T(8,128)(2,1)S(1)} all-to-all(bf16[8,48,1344]{2,1,0:T(8,128)(2,1)S(1)} %shard_map.105), channel_id=1, replica_groups=mesh['yh'=4,'zh'=6,'zl'=2,'core'=2,'x'=4,'yl'=2] {'x','yl'}, dimensions={0} | all-to-all | bytes 2064384 | tf_op jit(solution)/shard_map/all_to_all | solution.py:232
  89.1 4.4 %shard_map.106 = (bf16[384,768]{1,0:T(8,128)(2,1)}, bf16[3,224,768]{2,1,0:T(8,128)(2,1)}) custom-call(bf16[384,1344]{1,0:T(8,128)(2,1)S(1)} %bitcast.19, bf16[384,768]{1,0:T(8,128)(2,1)S(1)} %bitcast.25, bf16[384,768]{1,0:T(8,128)(2,1)S(1)} %bitcast.22, bf16[3,112,768]{2,1,0:T(8,128)(2,1)} %get-tuple-element.17.own_ref.own, ...), custom_call_target="tpu_custom_call" | custom-call | flops 924844032 | bytes 6000000 | tf_op jit(solution)/shard_map/pallas_call | solution.py:235
  93.4 1.9 %collective-permute-start.3 = (bf16[3,224,768]{2,1,0:T(8,128)(2,1)}, bf16[3,224,768]{2,1,0:T(8,128)(2,1)}, u32[]{:S(2)}, u32[]{:S(2)}) collective-permute-start(bf16[3,224,768]{2,1,0:T(8,128)(2,1)} %get-tuple-element.20), channel_id=1, source_target_pairs={{0,8},{8,0},{1,9},{9,1},{2,10},{10,2},{3,11},{11,3},{4,12},{12,4},... | collective-permute-start | bytes 3096584 | tf_op jit(solution)/shard_map/ppermute | solution.py:251
  95.4 5.2 %all-to-all-start.4 = ((bf16[4,96,768]{2,1,0:T(8,128)(2,1)}), bf16[4,96,768]{2,1,0:T(8,128)(2,1)}, u32[]{:S(2)}, u32[]{:S(2)}) async-start(bf16[4,96,768]{2,1,0:T(8,128)(2,1)} %bitcast.29), calls=%async_computation.4 | async-start | bytes 1179648 | tf_op jit(solution)/shard_map/all_to_all | solution.py:252
  100.5 1.1 copy-done.3
  101.6 1.1 copy-done.6
  102.7 3.3 %shard_map.108 = (f32[3,112,768]{2,1,0:T(8,128)}, bf16[3,112,768]{2,1,0:T(8,128)(2,1)}) custom-call(bf16[384,1344]{1,0:T(8,128)(2,1)S(1)} %bitcast.20, bf16[384,768]{1,0:T(8,128)(2,1)S(1)} %bitcast.26, bf16[384,768]{1,0:T(8,128)(2,1)S(1)} %bitcast.23, bf16[3,224,768]{2,1,0:T(8,128)(2,1)} %collective-permute-done.3.near_ref), custom_call_target="tpu_custom_call" | custom-call | flops 792723456 | bytes 3244032 | tf_op jit(solution)/shard_map/pallas_call | solution.py:42
  105.9 4.1 %collective-permute-start.4 = (bf16[3,112,768]{2,1,0:T(8,128)(2,1)}, bf16[3,112,768]{2,1,0:T(8,128)(2,1)S(1)}, u32[]{:S(2)}, u32[]{:S(2)}) collective-permute-start(bf16[3,112,768]{2,1,0:T(8,128)(2,1)} %get-tuple-element.21), channel_id=1, source_target_pairs={{0,16},{16,0},{1,17},{17,1},{2,18},{18,2},{3,19},{19,3},{4,20},{20... | collective-permute-start | bytes 1548296 | tf_op jit(solution)/shard_map/ppermute | solution.py:262
  110.0 8.0 %all-to-all-done.4.parts_ref = bf16[4,96,768]{2,1,0:T(8,128)(2,1)} async-done(((bf16[4,96,768]{2,1,0:T(8,128)(2,1)}), bf16[4,96,768]{2,1,0:T(8,128)(2,1)}, u32[]{:S(2)}, u32[]{:S(2)}) %all-to-all-start.4) | async-done | bytes 589856 | tf_op jit(solution)/shard_map/all_to_all | solution.py:252
  118.0 1.8 %shard_map.107 = bf16[96,768]{1,0:T(8,128)(2,1)} custom-call(bf16[4,96,768]{2,1,0:T(8,128)(2,1)} %all-to-all-done.4.parts_ref), custom_call_target="tpu_custom_call" | custom-call | flops 294912 | bytes 589824 | tf_op jit(solution)/shard_map/pallas_call | solution.py:42
  119.8 2.7 %collective-permute-done.4 = bf16[3,112,768]{2,1,0:T(8,128)(2,1)S(1)} collective-permute-done((bf16[3,112,768]{2,1,0:T(8,128)(2,1)}, bf16[3,112,768]{2,1,0:T(8,128)(2,1)S(1)}, u32[]{:S(2)}, u32[]{:S(2)}) %collective-permute-start.4) | collective-permute-done | bytes 516128 | tf_op jit(solution)/shard_map/ppermute | solution.py:262
  122.5 10.9 %all-to-all-start.5 = ((bf16[6,16,768]{2,1,0:T(8,128)(2,1)}), bf16[6,16,768]{2,1,0:T(8,128)(2,1)S(1)}, u32[]{:S(2)}, u32[]{:S(2)}) async-start(bf16[6,16,768]{2,1,0:T(8,128)(2,1)} %bitcast.30), calls=%async_computation.5 | async-start | bytes 294912 | tf_op jit(solution)/shard_map/all_to_all | solution.py:265
  133.4 2.2 %add_bitcast_fusion = (f32[112,768]{1,0:T(8,128)}, f32[112,768]{1,0:T(8,128)}, f32[112,768]{1,0:T(8,128)}) fusion(f32[3,112,768]{2,1,0:T(8,128)} %get-tuple-element.24, bf16[3,112,768]{2,1,0:T(8,128)(2,1)S(1)} %collective-permute-done.4), kind=kLoop, calls=%fused_computation | loop fusion | flops 516096 | bytes 2580480 | tf_op jit(solution)/shard_map/add | solution.py:268
  135.6 9.2 %all-to-all-done.5.parts_ref = bf16[6,16,768]{2,1,0:T(8,128)(2,1)S(1)} async-done(((bf16[6,16,768]{2,1,0:T(8,128)(2,1)}), bf16[6,16,768]{2,1,0:T(8,128)(2,1)S(1)}, u32[]{:S(2)}, u32[]{:S(2)}) %all-to-all-start.5) | async-done | bytes 147488 | tf_op jit(solution)/shard_map/all_to_all | solution.py:265
  144.8 0.9 shard_map.109
  (23 shorter events, 1.2 us)
Async XLA Ops:
  0.6 45.1 %copy-start = (bf16[1536,768]{1,0:T(8,128)(2,1)S(1)}, bf16[1536,768]{1,0:T(8,128)(2,1)}, u32[]{:S(2)}) copy-start(bf16[1536,768]{1,0:T(8,128)(2,1)} %param.10) | copy-start | bytes 7077892
  29.5 13.8 %collective-permute-start = (bf16[3,112,768]{2,1,0:T(8,128)(2,1)}, bf16[3,112,768]{2,1,0:T(8,128)(2,1)}, u32[]{:S(2)}, u32[]{:S(2)}) collective-permute-start(bf16[3,112,768]{2,1,0:T(8,128)(2,1)} %get-tuple-element.17.own_ref.own), channel_id=1, source_target_pairs={{0,16},{16,0},{1,17},{17,1},{2,18},{18,2},{3,19},{19,3},{4,20},{20... | collective-permute-start | bytes 1548296 | tf_op jit(solution)/shard_map/ppermute | solution.py:216
  34.0 20.7 %all-to-all-start.1 = ((bf16[4,96,768]{2,1,0:T(8,128)(2,1)}), bf16[4,96,768]{2,1,0:T(8,128)(2,1)S(1)}, u32[]{:S(2)}, u32[]{:S(2)}) async-start(bf16[4,96,768]{2,1,0:T(8,128)(2,1)} %shard_map.103), calls=%async_computation.1 | async-start | bytes 1179648 | tf_op jit(solution)/shard_map/all_to_all | solution.py:219
  41.4 4.4 %collective-permute-start.1 = (bf16[3,112,768]{2,1,0:T(8,128)(2,1)}, bf16[3,112,768]{2,1,0:T(8,128)(2,1)}, u32[]{:S(2)}, u32[]{:S(2)}) collective-permute-start(bf16[3,112,768]{2,1,0:T(8,128)(2,1)} %get-tuple-element.17.own_ref.own), channel_id=1, source_target_pairs={{0,8},{8,0},{1,9},{9,1},{2,10},{10,2},{3,11},{11,3},{4,12},{12,4},... | collective-permute-start | bytes 1548296 | tf_op jit(solution)/shard_map/ppermute | solution.py:215
  43.3 11.4 %collective-permute-start.2 = (bf16[3,112,768]{2,1,0:T(8,128)(2,1)}, bf16[3,112,768]{2,1,0:T(8,128)(2,1)}, u32[]{:S(2)}, u32[]{:S(2)}) collective-permute-start(bf16[3,112,768]{2,1,0:T(8,128)(2,1)} %collective-permute-done.across_ref.across), channel_id=1, source_target_pairs={{0,8},{8,0},{1,9},{9,1},{2,10},{10,2},{3,11},{11,3},{4,12},{12,4},... | collective-permute-start | bytes 1548296 | tf_op jit(solution)/shard_map/ppermute | solution.py:218
  45.8 11.7 %copy-start.4 = (bf16[24,1,16,768]{3,2,1,0:T(8,128)(2,1)}, bf16[24,1,16,768]{3,2,1,0:T(8,128)(2,1)S(1)}, u32[]{:S(2)}) copy-start(bf16[24,1,16,768]{3,2,1,0:T(8,128)(2,1)S(1)} %constant_dynamic-slice_fusion) | copy-start | bytes 1769476
  54.7 2.8 %copy-start.1 = (bf16[4,96,768]{2,1,0:T(8,128)(2,1)}, bf16[4,96,768]{2,1,0:T(8,128)(2,1)S(1)}, u32[]{:S(2)}) copy-start(bf16[4,96,768]{2,1,0:T(8,128)(2,1)S(1)} %all-to-all-done.1) | copy-start | bytes 1769476
  74.6 14.4 %copy-start.2 = (bf16[4,96,768]{2,1,0:T(8,128)(2,1)S(1)}, bf16[4,96,768]{2,1,0:T(8,128)(2,1)}, u32[]{:S(2)}) copy-start(bf16[4,96,768]{2,1,0:T(8,128)(2,1)} %copy-done.1) | copy-start | bytes 1769476
  74.6 14.4 %copy-start.5 = (bf16[24,1,16,768]{3,2,1,0:T(8,128)(2,1)S(1)}, bf16[24,1,16,768]{3,2,1,0:T(8,128)(2,1)}, u32[]{:S(2)}) copy-start(bf16[24,1,16,768]{3,2,1,0:T(8,128)(2,1)} %copy-done.4) | copy-start | bytes 1769476
  93.4 7.1 %collective-permute-start.3 = (bf16[3,224,768]{2,1,0:T(8,128)(2,1)}, bf16[3,224,768]{2,1,0:T(8,128)(2,1)}, u32[]{:S(2)}, u32[]{:S(2)}) collective-permute-start(bf16[3,224,768]{2,1,0:T(8,128)(2,1)} %get-tuple-element.20), channel_id=1, source_target_pairs={{0,8},{8,0},{1,9},{9,1},{2,10},{10,2},{3,11},{11,3},{4,12},{12,4},... | collective-permute-start | bytes 3096584 | tf_op jit(solution)/shard_map/ppermute | solution.py:251
  95.4 22.6 %all-to-all-start.4 = ((bf16[4,96,768]{2,1,0:T(8,128)(2,1)}), bf16[4,96,768]{2,1,0:T(8,128)(2,1)}, u32[]{:S(2)}, u32[]{:S(2)}) async-start(bf16[4,96,768]{2,1,0:T(8,128)(2,1)} %bitcast.29), calls=%async_computation.4 | async-start | bytes 1179648 | tf_op jit(solution)/shard_map/all_to_all | solution.py:252
  100.5 1.1 copy-start.3
  101.6 1.1 copy-start.6
  105.9 16.6 %collective-permute-start.4 = (bf16[3,112,768]{2,1,0:T(8,128)(2,1)}, bf16[3,112,768]{2,1,0:T(8,128)(2,1)S(1)}, u32[]{:S(2)}, u32[]{:S(2)}) collective-permute-start(bf16[3,112,768]{2,1,0:T(8,128)(2,1)} %get-tuple-element.21), channel_id=1, source_target_pairs={{0,16},{16,0},{1,17},{17,1},{2,18},{18,2},{3,19},{19,3},{4,20},{20... | collective-permute-start | bytes 1548296 | tf_op jit(solution)/shard_map/ppermute | solution.py:262
  122.5 22.3 %all-to-all-start.5 = ((bf16[6,16,768]{2,1,0:T(8,128)(2,1)}), bf16[6,16,768]{2,1,0:T(8,128)(2,1)S(1)}, u32[]{:S(2)}, u32[]{:S(2)}) async-start(bf16[6,16,768]{2,1,0:T(8,128)(2,1)} %bitcast.30), calls=%async_computation.5 | async-start | bytes 294912 | tf_op jit(solution)/shard_map/all_to_all | solution.py:265
  133.4 11.4 %copy-start.7 = (bf16[128,768]{1,0:T(8,128)(2,1)S(1)}, bf16[128,768]{1,0:T(8,128)(2,1)}, u32[]{:S(2)}) copy-start(bf16[128,768]{1,0:T(8,128)(2,1)} %grad_ref.1) | copy-start | bytes 589828
  133.4 11.4 %copy-start.8 = (bf16[16,128]{1,0:T(8,128)(2,1)S(1)}, bf16[16,128]{1,0:T(8,128)(2,1)}, u32[]{:S(2)}) copy-start(bf16[16,128]{1,0:T(8,128)(2,1)} %get-tuple-element.23.placement_ref) | copy-start | bytes 12292

commit v3 on v2

--- a/solution.py
+++ b/solution.py
@@ -22,19 +22,6 @@
 
 VMEM = pltpu.VMEM
 HBM = pltpu.HBM
-
-
-def scratch_call(body, outs, scratch, flops, *args):
-    moved = sum(a.size * a.dtype.itemsize for a in args)
-    return pl.pallas_call(
-        body,
-        out_shape=outs,
-        in_specs=[pl.BlockSpec(memory_space=VMEM)] * len(args),
-        out_specs=[pl.BlockSpec(memory_space=VMEM)] * len(outs),
-        scratch_shapes=[VMEM(scratch, BF16)],
-        cost_estimate=pl.CostEstimate(flops=flops, bytes_accessed=moved, transcendentals=0),
-        compiler_params=pltpu.CompilerParams(vmem_limit_bytes=24 * 1024 * 1024),
-    )(*args)
 
 
 def kernel_call(body, outs, flops, *args):
@@ -106,14 +93,17 @@
         copies_ref[i] = value_ref[...]
 
 
-def pre_kernel(own_ref, across_ref, near_ref, diagonal_ref, saved_ref, gathered_ref, parts_ref, w_ref):
+def pre_kernel(own_ref, across_ref, near_ref, diagonal_ref, saved_ref, gathered_ref, parts_ref, w_hbm, w_ref, sem):
     units = own_ref.shape[1]
     group = 4 * units
     for k in range(3):
         for i, ref in enumerate((own_ref, across_ref, near_ref, diagonal_ref)):
             w_ref[k * group + i * units : k * group + (i + 1) * units] = ref[k]
+    store = pltpu.make_async_copy(w_ref.at[pl.ds(0, 2 * group)], w_hbm, sem.at[0])
+    store.start()
     parts_ref[:, : 2 * group] = dot(saved_ref[...], w_ref[: 2 * group], LANES).astype(BF16)
     parts_ref[:, 2 * group :] = dot(gathered_ref[...], w_ref[2 * group :], LANES).astype(BF16)
+    store.wait()
 
 
 def activation_kernel(parts_ref, copies_ref):
@@ -132,47 +122,40 @@
         copies_ref[i] = act
 
 
-def weight_grads(act_ref, saved_ref, gathered_ref, k, half):
+def columns_of(act_ref, k, members):
     group = act_ref.shape[1] // 3
-    start = k * group + half * group // 2
-    low = start // 128 * 128
-    high = min((start + group // 2 + 127) // 128 * 128, 3 * group)
-    part = dot(act_ref[:, low:high], (gathered_ref if k == 2 else saved_ref)[...], ROWS)
-    return part[start - low : start - low + group // 2]
-
-
-def slot_kernel(
-    act_ref, saved_ref, gathered_ref, own, across, near, diagonal, slot_hbm, sent_hbm, w_ref, slot_ref, sent_ref, in_sems, out_sems
-):
-    units = own.shape[1]
-    group = 4 * units
-    fetches = []
-    for k in range(2):
-        for i, piece in enumerate((own, across, near, diagonal)):
-            place = w_ref.at[pl.ds(k * group + i * units, units)]
-            fetches.append(pltpu.make_async_copy(piece.at[k], place, in_sems.at[4 * k + i]))
-    for fetch in fetches:
-        fetch.start()
-    stores = []
-    for k in range(3):
-        sent_ref[k] = weight_grads(act_ref, saved_ref, gathered_ref, k, 1).astype(BF16)
-        stores.append(pltpu.make_async_copy(sent_ref.at[k], sent_hbm.at[k], out_sems.at[k]))
-        stores[k].start()
-    for fetch in fetches:
-        fetch.wait()
-    slot_ref[...] = dot(act_ref[:, : 2 * group], w_ref[...], PLAIN).astype(BF16)
-    stores.append(pltpu.make_async_copy(slot_ref, slot_hbm, out_sems.at[3]))
-    stores[3].start()
+    units = group // 4
+    return [act_ref[:, k * group + i * units : k * group + (i + 1) * units] for i in members]
+
+
+def slot_kernel(act_ref, w_ref, slot_hbm, sent_hbm, slot_ref, sent_ref, out_sems):
+    group = w_ref.shape[0] // 2
+    units = group // 4
+    columns = [c for k in range(3) for c in columns_of(act_ref, k, (1, 3))]
+    spare = sent_ref.shape[1] - 6 * units
+    columns.append(jnp.zeros((act_ref.shape[0], spare), BF16))
+    sent_ref[...] = jnp.concatenate(columns, axis=1)
+    sent_store = pltpu.make_async_copy(sent_ref, sent_hbm, out_sems.at[0])
+    sent_store.start()
+    stores = [sent_store]
+    rows = act_ref.shape[0] // N_YH
+    for i in range(N_YH):
+        block = pl.ds(i * rows, rows)
+        slot_ref[block] = dot(act_ref[block, : 2 * group], w_ref[...], PLAIN).astype(BF16)
+        stores.append(pltpu.make_async_copy(slot_ref.at[block], slot_hbm.at[block], out_sems.at[1 + i]))
+        stores[-1].start()
     for store in stores:
         store.wait()
 
 
-def kept_kernel(act_ref, saved_ref, gathered_ref, near_ref, own_ref, sent_ref):
+def kept_kernel(act_ref, act_far_ref, saved_ref, saved_far_ref, gathered_ref, gathered_far_ref, own_ref, sent_ref):
     units = own_ref.shape[1]
     for k in range(3):
-        part = weight_grads(act_ref, saved_ref, gathered_ref, k, 0)
-        own_ref[k] = part[:units] + near_ref[k, :units].astype(F32)
-        sent_ref[k] = (part[units:] + near_ref[k, units:].astype(F32)).astype(BF16)
+        here, far = (gathered_ref, gathered_far_ref) if k == 2 else (saved_ref, saved_far_ref)
+        part = dot(jnp.concatenate(columns_of(act_ref, k, (0, 2)), axis=1), here[...], ROWS)
+        part += dot(act_far_ref[:, 2 * k * units : 2 * (k + 1) * units], far[...], ROWS)
+        own_ref[k] = part[:units]
+        sent_ref[k] = part[units:].astype(BF16)
 
 
 def sum_kernel(parts_ref, total_ref):
@@ -218,15 +201,25 @@
     diagonal = lax.ppermute(across, "core", SWAP)
     gathered = lax.all_to_all(copies, "yh", 0, 0, tiled=True).reshape(slots, width)
 
-    member = lax.axis_index("zl") * 2 + lax.axis_index("core")
-    saved = lax.dynamic_index_in_dim(
-        saved_inputs.reshape(N_FAR, 4, capacity, width), member, axis=1, keepdims=False
-    ).reshape(slots, width)
+    def slots_of(member):
+        rows = saved_inputs.reshape(N_FAR, 4, capacity, width)
+        return lax.dynamic_index_in_dim(rows, member, axis=1, keepdims=False).reshape(slots, width)
+
+    chip, core = lax.axis_index("zl"), lax.axis_index("core")
+    saved = slots_of(chip * 2 + core)
+    saved_far = slots_of((1 - chip) * 2 + core)
 
     pieces = (own, across, near, diagonal)
-    (parts,) = scratch_call(
-        pre_kernel, [array(slots, 3 * group)], (3 * group, width), 6 * slots * group * width, *pieces, saved, gathered
-    )
+    parts, w_both = pl.pallas_call(
+        pre_kernel,
+        out_shape=[array(slots, 3 * group), HBM((2 * group, width), BF16)],
+        in_specs=[pl.BlockSpec(memory_space=VMEM)] * 6,
+        out_specs=[pl.BlockSpec(memory_space=VMEM), pl.BlockSpec(memory_space=pl.ANY)],
+        scratch_shapes=[VMEM((3 * group, width), BF16), pltpu.SemaphoreType.DMA((1,))],
+        cost_estimate=pl.CostEstimate(flops=6 * slots * group * width, bytes_accessed=4000000, transcendentals=0),
+        compiler_params=pltpu.CompilerParams(vmem_limit_bytes=24 * 1024 * 1024),
+    )(*pieces, saved, gathered)
+    gathered_far = lax.ppermute(gathered, "zl", SWAP)
     parts = lax.all_to_all(parts.reshape(N_EP, slots // N_EP, 3 * group), EP, 0, 0, tiled=True)
     (copies,) = kernel_call(activation_kernel, [array(*parts.shape)], 20 * parts.size, parts)
     act = lax.all_to_all(copies, EP, 0, 0, tiled=True)
@@ -234,38 +227,37 @@
 
     slot_part, sent = pl.pallas_call(
         slot_kernel,
-        out_shape=[HBM((slots, width), BF16), HBM((3, 2 * units, width), BF16)],
-        in_specs=[pl.BlockSpec(memory_space=VMEM)] * 3 + [pl.BlockSpec(memory_space=pl.ANY)] * 4,
+        out_shape=[HBM((slots, width), BF16), HBM((slots, width), BF16)],
+        in_specs=[pl.BlockSpec(memory_space=VMEM)] * 2,
         out_specs=[pl.BlockSpec(memory_space=pl.ANY)] * 2,
         scratch_shapes=[
-            VMEM((2 * group, width), BF16),
             VMEM((slots, width), BF16),
-            VMEM((3, 2 * units, width), BF16),
-            pltpu.SemaphoreType.DMA((8,)),
-            pltpu.SemaphoreType.DMA((4,)),
+            VMEM((slots, width), BF16),
+            pltpu.SemaphoreType.DMA((1 + N_YH,)),
         ],
-        cost_estimate=pl.CostEstimate(flops=7 * slots * group * width, bytes_accessed=6000000, transcendentals=0),
+        cost_estimate=pl.CostEstimate(flops=4 * slots * group * width, bytes_accessed=6000000, transcendentals=0),
         compiler_params=pltpu.CompilerParams(vmem_limit_bytes=24 * 1024 * 1024),
-    )(act, saved, gathered, *pieces)
-
-    from_near = lax.ppermute(sent, "core", SWAP)
+    )(act, w_both)
+
+    act_far = lax.ppermute(sent, "zl", SWAP)
     slot_part = lax.all_to_all(slot_part.reshape(N_YH, N_ZH * capacity, width), "yh", 0, 0, tiled=True)
     kept, sent = kernel_call(
         kept_kernel,
         [HBM((3, units, width), F32), HBM((3, units, width), BF16)],
         6 * slots * group * width,
         act,
+        act_far,
         saved,
+        saved_far,
         gathered,
-        from_near,
+        gathered_far,
     )
-    from_across = lax.ppermute(sent, "zl", SWAP)
+    from_near = lax.ppermute(sent, "core", SWAP)
     (slot_part,) = kernel_call(sum_kernel, [HBM((N_ZH * capacity, width), BF16)], slot_part.size, slot_part)
-    slot_part, from_across = lax.optimization_barrier((slot_part, from_across))
     slot_part = lax.all_to_all(slot_part.reshape(N_ZH, capacity, width), "zh", 0, 0, tiled=True)
     (grad_in,) = kernel_call(result_kernel, [array(tokens, width)], tokens * width * 32, slot_part, placement, grad_out)
 
-    grad_gate, grad_up, grad_down = [kept[k] + from_across[k].astype(F32) for k in range(3)]
+    grad_gate, grad_up, grad_down = [kept[k] + from_near[k].astype(F32) for k in range(3)]
     return (grad_in, grad_gate, grad_up, grad_down)
 
 

time: 147 us -> 142 us (0.966)
  blocking collectives: 57.8 us -> 43.5 us
  starting transfers between devices: 37.4 us -> 46.1 us
  waiting for transfers between devices: 28.7 us -> 32.2 us
  Pallas kernels: 16.5 us -> 14.8 us
    all_to_all x1 -> x0, blocking collectives: 14.4 us -> none  [local(): act = lax.all_to_all(copies, EP, 0, 0, tiled=True)]
    all_to_all x0 -> x1, waiting for transfers between devices: none -> 8.48 us  [local(): act = lax.all_to_all(copies, EP, 0, 0, tiled=True)]
    all_to_all x1, waiting for transfers between devices: 7.99 us -> 0.01 us  [local(): lax.all_to_all(slot_part.reshape(N_YH, N_ZH * capacity, width), 'yh', 0,...]
    ppermute x1 -> x2, starting transfers between devices: 4.1 us -> 8.16 us  [the longest x1 4.41 us: local(): act_far = lax.ppermute(sent, 'zl', SWAP)]
    all_to_all x0 -> x1, starting transfers between devices: none -> 3.56 us  [local(): act = lax.all_to_all(copies, EP, 0, 0, tiled=True)]
    pallas_call x2, Pallas kernels: 7.19 us -> 4.81 us  [the longest x1 3.04 us: local(): pl.pallas_call(pre_kernel, out_shape=[array(slots, 3 * group), HBM((2 * g...]
    ppermute x1 -> x2, waiting for transfers between devices: 2.68 us -> 5.04 us  [the longest x1 5.04 us: local(): act_far = lax.ppermute(sent, 'zl', SWAP)]
    all_to_all x1, waiting for transfers between devices: 9.17 us -> 11.1 us  [local(): lax.all_to_all(slot_part.reshape(N_ZH, capacity, width), 'zh', 0, 0, tile...]
  transfers between devices with their start and end apart: 8 -> 10, of which waited for: 4 -> 4; matrix products, arithmetic and copies ran while one was open for 2% -> 2% of each run, Pallas kernels for 4% -> 5%
where the time goes in v3:
time: 142 us; the launch traced here: 141 us
  starting transfers between devices  46.1 us (32%)
  blocking collectives  43.5 us (31%)
  waiting for transfers between devices  32.2 us (23%)
  Pallas kernels  14.8 us (10%)
  local copies, waits for them, and re-layouts  2.69 us (2%)
    all_to_all x1, blocking collectives, local(): lax.all_to_all(copies, 'zh', 0, 0, tiled=True)  26.7 us
    all_to_all x1, blocking collectives, local(): lax.all_to_all(parts.reshape(N_EP, slots // N_EP, 3 * group), EP, 0, 0, t...  16.8 us
    all_to_all x1, starting transfers between devices, local(): lax.all_to_all(slot_part.reshape(N_ZH, capacity, width), 'zh', 0, 0, tile...  12.8 us
    all_to_all x1, waiting for transfers between devices, local(): lax.all_to_all(slot_part.reshape(N_ZH, capacity, width), 'zh', 0, 0, tile...  11.1 us
    all_to_all x1, waiting for transfers between devices, local(): act = lax.all_to_all(copies, EP, 0, 0, tiled=True)  8.48 us
    pallas_call x5, Pallas kernels, kernel_call(): pl.pallas_call(body, out_shape=outs, in_specs=[pl.BlockSpec(memory_space=...  7.83 us
    all_to_all x1, waiting for transfers between devices, local(): lax.all_to_all(copies, 'yh', 0, 0, tiled=True).reshape(slots, width)  7.6 us
    all_to_all x1, starting transfers between devices, local(): lax.all_to_all(copies, 'yh', 0, 0, tiled=True).reshape(slots, width)  7.43 us
  transfers between devices with their start and end apart: 10, of which 4 were waited for; matrix products, arithmetic and copies ran while one was open for 2% of the time, Pallas kernels for 5%

profile of v3, /device:TPU:16, one launch (start us, length us, event | category | flops | bytes accessed | tf_op | source)
XLA Modules:
  0.0 141.1 jit_solution(3687649141092404372)
XLA Ops:
  0.6 2.1 %shard_map.102 = (bf16[6,16,768]{2,1,0:T(8,128)(2,1)}, bf16[16,128]{1,0:T(8,128)(2,1)}, bf16[3,112,768]{2,1,0:T(8,128)(2,1)}) custom-call(bf16[128,768]{1,0:T(8,128)(2,1)} %grad_ref.1, s32[4,128]{1,0:T(4,128)} %bitcast.34, f32[4,128]{1,0:T(4,128)} %bitcast.35, bf16[112,768]{1,0:T(8,128)(2,1)} %wg_hbm.1, bf16[112,768]{1,0:T(8,128)(2,1)} %wu_hbm.1, ...), custom_call_target="tpu_custom_call" | custom-call | tf_op jit(solution)/shard_map/pallas_call | solution.py:183
  2.8 26.7 %all_to_all.30 = bf16[6,16,768]{2,1,0:T(8,128)(2,1)S(1)} all-to-all(bf16[6,16,768]{2,1,0:T(8,128)(2,1)} %get-tuple-element.15), channel_id=1, replica_groups=mesh['yh'=4,'zh'=6,'zl'=2,'core'=2,'x'=4,'yl'=2] {'zh'}, dimensions={0} | all-to-all | bytes 294912 | tf_op jit(solution)/shard_map/all_to_all | solution.py:196
  29.5 3.6 %collective-permute-start = (bf16[3,112,768]{2,1,0:T(8,128)(2,1)}, bf16[3,112,768]{2,1,0:T(8,128)(2,1)S(1)}, u32[]{:S(2)}, u32[]{:S(2)}) collective-permute-start(bf16[3,112,768]{2,1,0:T(8,128)(2,1)} %get-tuple-element.17.own_ref), channel_id=1, source_target_pairs={{0,16},{16,0},{1,17},{17,1},{2,18},{18,2},{3,19},{19,3},{4,20},{20... | collective-permute-start | bytes 1548296 | tf_op jit(solution)/shard_map/ppermute | solution.py:199
  34.0 7.4 %all-to-all-start.1 = ((bf16[4,96,768]{2,1,0:T(8,128)(2,1)}), bf16[4,96,768]{2,1,0:T(8,128)(2,1)S(1)}, u32[]{:S(2)}, u32[]{:S(2)}) async-start(bf16[4,96,768]{2,1,0:T(8,128)(2,1)} %shard_map.103), calls=%async_computation.1 | async-start | bytes 1179648 | tf_op jit(solution)/shard_map/all_to_all | solution.py:202
  41.4 1.9 %collective-permute-start.1 = (bf16[3,112,768]{2,1,0:T(8,128)(2,1)S(1)}, bf16[3,112,768]{2,1,0:T(8,128)(2,1)S(1)}, u32[]{:S(2)}, u32[]{:S(2)}) collective-permute-start(bf16[3,112,768]{2,1,0:T(8,128)(2,1)S(1)} %copy-done.2), channel_id=1, source_target_pairs={{0,8},{8,0},{1,9},{9,1},{2,10},{10,2},{3,11},{11,3},{4,12},{12,4},... | collective-permute-start | bytes 1548296 | tf_op jit(solution)/shard_map/ppermute | solution.py:198
  43.3 2.4 %collective-permute-start.2 = (bf16[3,112,768]{2,1,0:T(8,128)(2,1)S(1)}, bf16[3,112,768]{2,1,0:T(8,128)(2,1)}, u32[]{:S(2)}, u32[]{:S(2)}) collective-permute-start(bf16[3,112,768]{2,1,0:T(8,128)(2,1)S(1)} %collective-permute-done.across_ref), channel_id=1, source_target_pairs={{0,8},{8,0},{1,9},{9,1},{2,10},{10,2},{3,11},{11,3},{4,12},{12,4},... | collective-permute-start | bytes 1548296 | tf_op jit(solution)/shard_map/ppermute | solution.py:201
  45.8 1.3 constant_dynamic-slice_fusion
  47.1 7.6 %all-to-all-done.1 = bf16[4,96,768]{2,1,0:T(8,128)(2,1)S(1)} async-done(((bf16[4,96,768]{2,1,0:T(8,128)(2,1)}), bf16[4,96,768]{2,1,0:T(8,128)(2,1)S(1)}, u32[]{:S(2)}, u32[]{:S(2)}) %all-to-all-start.1) | async-done | bytes 589856 | tf_op jit(solution)/shard_map/all_to_all | solution.py:202
  54.7 3.0 %shard_map.104 = (bf16[384,1344]{1,0:T(8,128)(2,1)S(1)}, bf16[896,768]{1,0:T(8,128)(2,1)}) custom-call(bf16[3,112,768]{2,1,0:T(8,128)(2,1)S(1)} %copy-done.2, bf16[3,112,768]{2,1,0:T(8,128)(2,1)S(1)} %collective-permute-done.across_ref, bf16[3,112,768]{2,1,0:T(8,128)(2,1)S(1)} %collective-permute-done.1.near_ref, ...), custom_call_target="tpu_custom_call" | custom-call | flops 792723456 | bytes 4000000 | tf_op jit(solution)/shard_map/pallas_call | solution.py:213
  57.8 16.8 %all_to_all.31.parts_ref = bf16[8,48,1344]{2,1,0:T(8,128)(2,1)S(1)} all-to-all(bf16[8,48,1344]{2,1,0:T(8,128)(2,1)S(1)} %bitcast.29), channel_id=1, replica_groups=mesh['yh'=4,'zh'=6,'zl'=2,'core'=2,'x'=4,'yl'=2] {'x','yl'}, dimensions={0} | all-to-all | bytes 2064384 | tf_op jit(solution)/shard_map/all_to_all | solution.py:223
  74.6 1.2 shard_map.105
  75.8 3.6 %all-to-all-start.3 = ((bf16[8,48,1344]{2,1,0:T(8,128)(2,1)}), bf16[8,48,1344]{2,1,0:T(8,128)(2,1)S(1)}, u32[]{:S(2)}, u32[]{:S(2)}) async-start(bf16[8,48,1344]{2,1,0:T(8,128)(2,1)} %shard_map.105), calls=%async_computation.3 | async-start | bytes 2162688 | tf_op jit(solution)/shard_map/all_to_all | solution.py:225
  79.4 3.8 %collective-permute-start.4 = (bf16[384,768]{1,0:T(8,128)(2,1)S(1)}, bf16[384,768]{1,0:T(8,128)(2,1)}, u32[]{:S(2)}, u32[]{:S(2)}) collective-permute-start(bf16[384,768]{1,0:T(8,128)(2,1)S(1)} %bitcast.24), channel_id=1, source_target_pairs={{0,16},{16,0},{1,17},{17,1},{2,18},{18,2},{3,19},{19,3},{4,20},{20... | collective-permute-start | bytes 1769480 | tf_op jit(solution)/shard_map/ppermute | solution.py:222
  83.1 8.5 %all-to-all-done.3 = bf16[8,48,1344]{2,1,0:T(8,128)(2,1)S(1)} async-done(((bf16[8,48,1344]{2,1,0:T(8,128)(2,1)}), bf16[8,48,1344]{2,1,0:T(8,128)(2,1)S(1)}, u32[]{:S(2)}, u32[]{:S(2)}) %all-to-all-start.3) | async-done | bytes 1032224 | tf_op jit(solution)/shard_map/all_to_all | solution.py:225
  91.6 1.3 copy-done
  93.0 1.8 %shard_map.106 = (bf16[384,768]{1,0:T(8,128)(2,1)}, bf16[384,768]{1,0:T(8,128)(2,1)}) custom-call(bf16[384,1344]{1,0:T(8,128)(2,1)S(1)} %bitcast.21, bf16[896,768]{1,0:T(8,128)(2,1)S(1)} %copy-done), custom_call_target="tpu_custom_call" | custom-call | flops 528482304 | bytes 6000000 | tf_op jit(solution)/shard_map/pallas_call | solution.py:228
  94.7 4.4 %collective-permute-start.3 = (bf16[384,768]{1,0:T(8,128)(2,1)}, bf16[384,768]{1,0:T(8,128)(2,1)}, u32[]{:S(2)}, u32[]{:S(2)}) collective-permute-start(bf16[384,768]{1,0:T(8,128)(2,1)} %get-tuple-element.23), channel_id=1, source_target_pairs={{0,16},{16,0},{1,17},{17,1},{2,18},{18,2},{3,19},{19,3},{4,20},{20... | collective-permute-start | bytes 1769480 | tf_op jit(solution)/shard_map/ppermute | solution.py:242
  99.1 4.2 %all-to-all-start.4 = ((bf16[4,96,768]{2,1,0:T(8,128)(2,1)}), bf16[4,96,768]{2,1,0:T(8,128)(2,1)S(1)}, u32[]{:S(2)}, u32[]{:S(2)}) async-start(bf16[4,96,768]{2,1,0:T(8,128)(2,1)} %bitcast.32), calls=%async_computation.4 | async-start | bytes 1179648 | tf_op jit(solution)/shard_map/all_to_all | solution.py:243
  103.4 5.0 %collective-permute-done.3.act_far_ref = bf16[384,768]{1,0:T(8,128)(2,1)} collective-permute-done((bf16[384,768]{1,0:T(8,128)(2,1)}, bf16[384,768]{1,0:T(8,128)(2,1)}, u32[]{:S(2)}, u32[]{:S(2)}) %collective-permute-start.3) | collective-permute-done | bytes 589856 | tf_op jit(solution)/shard_map/ppermute | solution.py:242
  108.4 4.1 %shard_map.109 = (f32[3,112,768]{2,1,0:T(8,128)}, bf16[3,112,768]{2,1,0:T(8,128)(2,1)}) custom-call(bf16[384,1344]{1,0:T(8,128)(2,1)S(1)} %bitcast.22, bf16[384,768]{1,0:T(8,128)(2,1)} %collective-permute-done.3.act_far_ref, bf16[384,768]{1,0:T(8,128)(2,1)S(1)} %bitcast.27, bf16[384,768]{1,0:T(8,128)(2,1)S(1)} %bitcast.28, bf16[384,768]{1,0:T(8,128)(2,1)S(1)} %bitcast.25, ...), custom_call_target="tpu_custom_call" | custom-call | flops 792723456 | bytes 3981312 | tf_op jit(solution)/shard_map/pallas_call | solution.py:29
  112.5 2.0 %collective-permute-start.5 = (bf16[3,112,768]{2,1,0:T(8,128)(2,1)}, bf16[3,112,768]{2,1,0:T(8,128)(2,1)S(1)}, u32[]{:S(2)}, u32[]{:S(2)}) collective-permute-start(bf16[3,112,768]{2,1,0:T(8,128)(2,1)} %get-tuple-element.25), channel_id=1, source_target_pairs={{0,8},{8,0},{1,9},{9,1},{2,10},{10,2},{3,11},{11,3},{4,12},{12,4},... | collective-permute-start | bytes 1548296 | tf_op jit(solution)/shard_map/ppermute | solution.py:255
  115.3 12.8 %all-to-all-start.5 = ((bf16[6,16,768]{2,1,0:T(8,128)(2,1)}), bf16[6,16,768]{2,1,0:T(8,128)(2,1)S(1)}, u32[]{:S(2)}, u32[]{:S(2)}) async-start(bf16[6,16,768]{2,1,0:T(8,128)(2,1)} %bitcast.33), calls=%async_computation.5 | async-start | bytes 294912 | tf_op jit(solution)/shard_map/all_to_all | solution.py:257
  128.1 1.0 add_bitcast_fusion
  129.1 11.1 %all-to-all-done.5.parts_ref = bf16[6,16,768]{2,1,0:T(8,128)(2,1)S(1)} async-done(((bf16[6,16,768]{2,1,0:T(8,128)(2,1)}), bf16[6,16,768]{2,1,0:T(8,128)(2,1)S(1)}, u32[]{:S(2)}, u32[]{:S(2)}) %all-to-all-start.5) | async-done | bytes 147488 | tf_op jit(solution)/shard_map/all_to_all | solution.py:257
  (18 shorter events, 2.6 us)
Async XLA Ops:
  2.8 38.6 %copy-start.2 = (bf16[3,112,768]{2,1,0:T(8,128)(2,1)S(1)}, bf16[3,112,768]{2,1,0:T(8,128)(2,1)}, u32[]{:S(2)}) copy-start(bf16[3,112,768]{2,1,0:T(8,128)(2,1)} %get-tuple-element.17.own_ref) | copy-start | bytes 1548292
  29.5 13.8 %collective-permute-start = (bf16[3,112,768]{2,1,0:T(8,128)(2,1)}, bf16[3,112,768]{2,1,0:T(8,128)(2,1)S(1)}, u32[]{:S(2)}, u32[]{:S(2)}) collective-permute-start(bf16[3,112,768]{2,1,0:T(8,128)(2,1)} %get-tuple-element.17.own_ref), channel_id=1, source_target_pairs={{0,16},{16,0},{1,17},{17,1},{2,18},{18,2},{3,19},{19,3},{4,20},{20... | collective-permute-start | bytes 1548296 | tf_op jit(solution)/shard_map/ppermute | solution.py:199
  34.0 20.7 %all-to-all-start.1 = ((bf16[4,96,768]{2,1,0:T(8,128)(2,1)}), bf16[4,96,768]{2,1,0:T(8,128)(2,1)S(1)}, u32[]{:S(2)}, u32[]{:S(2)}) async-start(bf16[4,96,768]{2,1,0:T(8,128)(2,1)} %shard_map.103), calls=%async_computation.1 | async-start | bytes 1179648 | tf_op jit(solution)/shard_map/all_to_all | solution.py:202
  41.4 5.7 %collective-permute-start.1 = (bf16[3,112,768]{2,1,0:T(8,128)(2,1)S(1)}, bf16[3,112,768]{2,1,0:T(8,128)(2,1)S(1)}, u32[]{:S(2)}, u32[]{:S(2)}) collective-permute-start(bf16[3,112,768]{2,1,0:T(8,128)(2,1)S(1)} %copy-done.2), channel_id=1, source_target_pairs={{0,8},{8,0},{1,9},{9,1},{2,10},{10,2},{3,11},{11,3},{4,12},{12,4},... | collective-permute-start | bytes 1548296 | tf_op jit(solution)/shard_map/ppermute | solution.py:198
  43.3 11.4 %collective-permute-start.2 = (bf16[3,112,768]{2,1,0:T(8,128)(2,1)S(1)}, bf16[3,112,768]{2,1,0:T(8,128)(2,1)}, u32[]{:S(2)}, u32[]{:S(2)}) collective-permute-start(bf16[3,112,768]{2,1,0:T(8,128)(2,1)S(1)} %collective-permute-done.across_ref), channel_id=1, source_target_pairs={{0,8},{8,0},{1,9},{9,1},{2,10},{10,2},{3,11},{11,3},{4,12},{12,4},... | collective-permute-start | bytes 1548296 | tf_op jit(solution)/shard_map/ppermute | solution.py:201
  75.8 15.8 %all-to-all-start.3 = ((bf16[8,48,1344]{2,1,0:T(8,128)(2,1)}), bf16[8,48,1344]{2,1,0:T(8,128)(2,1)S(1)}, u32[]{:S(2)}, u32[]{:S(2)}) async-start(bf16[8,48,1344]{2,1,0:T(8,128)(2,1)} %shard_map.105), calls=%async_computation.3 | async-start | bytes 2162688 | tf_op jit(solution)/shard_map/all_to_all | solution.py:225
  79.4 24.0 %collective-permute-start.4 = (bf16[384,768]{1,0:T(8,128)(2,1)S(1)}, bf16[384,768]{1,0:T(8,128)(2,1)}, u32[]{:S(2)}, u32[]{:S(2)}) collective-permute-start(bf16[384,768]{1,0:T(8,128)(2,1)S(1)} %bitcast.24), channel_id=1, source_target_pairs={{0,16},{16,0},{1,17},{17,1},{2,18},{18,2},{3,19},{19,3},{4,20},{20... | collective-permute-start | bytes 1769480 | tf_op jit(solution)/shard_map/ppermute | solution.py:222
  91.6 1.3 copy-start
  94.7 13.7 %collective-permute-start.3 = (bf16[384,768]{1,0:T(8,128)(2,1)}, bf16[384,768]{1,0:T(8,128)(2,1)}, u32[]{:S(2)}, u32[]{:S(2)}) collective-permute-start(bf16[384,768]{1,0:T(8,128)(2,1)} %get-tuple-element.23), channel_id=1, source_target_pairs={{0,16},{16,0},{1,17},{17,1},{2,18},{18,2},{3,19},{19,3},{4,20},{20... | collective-permute-start | bytes 1769480 | tf_op jit(solution)/shard_map/ppermute | solution.py:242
  99.1 15.4 %all-to-all-start.4 = ((bf16[4,96,768]{2,1,0:T(8,128)(2,1)}), bf16[4,96,768]{2,1,0:T(8,128)(2,1)S(1)}, u32[]{:S(2)}, u32[]{:S(2)}) async-start(bf16[4,96,768]{2,1,0:T(8,128)(2,1)} %bitcast.32), calls=%async_computation.4 | async-start | bytes 1179648 | tf_op jit(solution)/shard_map/all_to_all | solution.py:243
  112.5 15.6 %copy-start.4 = (f32[3,112,768]{2,1,0:T(8,128)S(1)}, f32[3,112,768]{2,1,0:T(8,128)}, u32[]{:S(2)}) copy-start(f32[3,112,768]{2,1,0:T(8,128)} %get-tuple-element.24) | copy-start | bytes 3096580
  112.5 15.6 %collective-permute-start.5 = (bf16[3,112,768]{2,1,0:T(8,128)(2,1)}, bf16[3,112,768]{2,1,0:T(8,128)(2,1)S(1)}, u32[]{:S(2)}, u32[]{:S(2)}) collective-permute-start(bf16[3,112,768]{2,1,0:T(8,128)(2,1)} %get-tuple-element.25), channel_id=1, source_target_pairs={{0,8},{8,0},{1,9},{9,1},{2,10},{10,2},{3,11},{11,3},{4,12},{12,4},... | collective-permute-start | bytes 1548296 | tf_op jit(solution)/shard_map/ppermute | solution.py:255
  115.3 24.9 %all-to-all-start.5 = ((bf16[6,16,768]{2,1,0:T(8,128)(2,1)}), bf16[6,16,768]{2,1,0:T(8,128)(2,1)S(1)}, u32[]{:S(2)}, u32[]{:S(2)}) async-start(bf16[6,16,768]{2,1,0:T(8,128)(2,1)} %bitcast.33), calls=%async_computation.5 | async-start | bytes 294912 | tf_op jit(solution)/shard_map/all_to_all | solution.py:257
  128.1 12.1 %copy-start.1 = (bf16[128,768]{1,0:T(8,128)(2,1)S(1)}, bf16[128,768]{1,0:T(8,128)(2,1)}, u32[]{:S(2)}) copy-start(bf16[128,768]{1,0:T(8,128)(2,1)} %grad_ref.1) | copy-start | bytes 589828
  128.1 12.1 %copy-start.3 = (bf16[16,128]{1,0:T(8,128)(2,1)S(1)}, bf16[16,128]{1,0:T(8,128)(2,1)}, u32[]{:S(2)}) copy-start(bf16[16,128]{1,0:T(8,128)(2,1)} %get-tuple-element.22.placement_ref) | copy-start | bytes 12292

commit v4 on v3

--- a/solution.py
+++ b/solution.py
@@ -128,32 +128,36 @@
     return [act_ref[:, k * group + i * units : k * group + (i + 1) * units] for i in members]
 
 
-def slot_kernel(act_ref, w_ref, slot_hbm, sent_hbm, slot_ref, sent_ref, out_sems):
-    group = w_ref.shape[0] // 2
-    units = group // 4
+def pack_kernel(act_ref, sent_ref):
     columns = [c for k in range(3) for c in columns_of(act_ref, k, (1, 3))]
-    spare = sent_ref.shape[1] - 6 * units
+    spare = sent_ref.shape[1] - act_ref.shape[1] // 2
     columns.append(jnp.zeros((act_ref.shape[0], spare), BF16))
     sent_ref[...] = jnp.concatenate(columns, axis=1)
-    sent_store = pltpu.make_async_copy(sent_ref, sent_hbm, out_sems.at[0])
-    sent_store.start()
-    stores = [sent_store]
+
+
+def slot_kernel(act_ref, w_ref, slot_hbm, slot_ref, sems):
+    stores = []
     rows = act_ref.shape[0] // N_YH
     for i in range(N_YH):
         block = pl.ds(i * rows, rows)
-        slot_ref[block] = dot(act_ref[block, : 2 * group], w_ref[...], PLAIN).astype(BF16)
-        stores.append(pltpu.make_async_copy(slot_ref.at[block], slot_hbm.at[block], out_sems.at[1 + i]))
+        slot_ref[block] = dot(act_ref[block, : w_ref.shape[0]], w_ref[...], PLAIN).astype(BF16)
+        stores.append(pltpu.make_async_copy(slot_ref.at[block], slot_hbm.at[block], sems.at[i]))
         stores[-1].start()
     for store in stores:
         store.wait()
 
 
-def kept_kernel(act_ref, act_far_ref, saved_ref, saved_far_ref, gathered_ref, gathered_far_ref, own_ref, sent_ref):
+def near_kernel(act_ref, saved_ref, gathered_ref, part_ref):
+    for k in range(3):
+        here = gathered_ref if k == 2 else saved_ref
+        part_ref[k] = dot(jnp.concatenate(columns_of(act_ref, k, (0, 2)), axis=1), here[...], ROWS)
+
+
+def far_kernel(act_ref, saved_ref, gathered_ref, part_ref, own_ref, sent_ref):
     units = own_ref.shape[1]
     for k in range(3):
-        here, far = (gathered_ref, gathered_far_ref) if k == 2 else (saved_ref, saved_far_ref)
-        part = dot(jnp.concatenate(columns_of(act_ref, k, (0, 2)), axis=1), here[...], ROWS)
-        part += dot(act_far_ref[:, 2 * k * units : 2 * (k + 1) * units], far[...], ROWS)
+        far = gathered_ref if k == 2 else saved_ref
+        part = part_ref[k] + dot(act_ref[:, 2 * k * units : 2 * (k + 1) * units], far[...], ROWS)
         own_ref[k] = part[:units]
         sent_ref[k] = part[units:].astype(BF16)
 
@@ -225,32 +229,30 @@
     act = lax.all_to_all(copies, EP, 0, 0, tiled=True)
     act = act.reshape(slots, 3 * group)
 
-    slot_part, sent = pl.pallas_call(
+    (sent,) = kernel_call(pack_kernel, [HBM((slots, width), BF16)], act.size, act)
+    act_far = lax.ppermute(sent, "zl", SWAP)
+    slot_part = pl.pallas_call(
         slot_kernel,
-        out_shape=[HBM((slots, width), BF16), HBM((slots, width), BF16)],
+        out_shape=HBM((slots, width), BF16),
         in_specs=[pl.BlockSpec(memory_space=VMEM)] * 2,
-        out_specs=[pl.BlockSpec(memory_space=pl.ANY)] * 2,
-        scratch_shapes=[
-            VMEM((slots, width), BF16),
-            VMEM((slots, width), BF16),
-            pltpu.SemaphoreType.DMA((1 + N_YH,)),
-        ],
-        cost_estimate=pl.CostEstimate(flops=4 * slots * group * width, bytes_accessed=6000000, transcendentals=0),
+        out_specs=pl.BlockSpec(memory_space=pl.ANY),
+        scratch_shapes=[VMEM((slots, width), BF16), pltpu.SemaphoreType.DMA((N_YH,))],
+        cost_estimate=pl.CostEstimate(flops=4 * slots * group * width, bytes_accessed=3000000, transcendentals=0),
         compiler_params=pltpu.CompilerParams(vmem_limit_bytes=24 * 1024 * 1024),
     )(act, w_both)
 
-    act_far = lax.ppermute(sent, "zl", SWAP)
     slot_part = lax.all_to_all(slot_part.reshape(N_YH, N_ZH * capacity, width), "yh", 0, 0, tiled=True)
+    (part,) = kernel_call(
+        near_kernel, [array(3, 2 * units, width, dtype=F32)], 3 * slots * group * width, act, saved, gathered
+    )
     kept, sent = kernel_call(
-        kept_kernel,
+        far_kernel,
         [HBM((3, units, width), F32), HBM((3, units, width), BF16)],
-        6 * slots * group * width,
-        act,
+        3 * slots * group * width,
         act_far,
-        saved,
         saved_far,
-        gathered,
         gathered_far,
+        part,
     )
     from_near = lax.ppermute(sent, "core", SWAP)
     (slot_part,) = kernel_call(sum_kernel, [HBM((N_ZH * capacity, width), BF16)], slot_part.size, slot_part)

time: 142 us -> 140 us (0.986)
  waiting for transfers between devices: 32.2 us -> 30.2 us
    ppermute x1, waiting for transfers between devices: 5.04 us -> 2.27 us  [local(): act_far = lax.ppermute(sent, 'zl', SWAP)]
    all_to_all x1, waiting for transfers between devices: 0.01 us -> 1.44 us  [local(): lax.all_to_all(slot_part.reshape(N_YH, N_ZH * capacity, width), 'yh', 0,...]
    pallas_call x5 -> x7, Pallas kernels: 7.83 us -> 9.07 us  [kernel_call(): pl.pallas_call(body, out_shape=outs, in_specs=[pl.BlockSpec(memory_space=...]
  transfers between devices with their start and end apart: 10 -> 10, of which waited for: 4 -> 5; matrix products, arithmetic and copies ran while one was open for 2% -> 2% of each run, Pallas kernels for 5% -> 6%
where the time goes in v4:
time: 140 us; the launch traced here: 139 us
  starting transfers between devices  46.5 us (33%)
  blocking collectives  43.5 us (31%)
  waiting for transfers between devices  30.2 us (22%)
  Pallas kernels  16 us (11%)
    all_to_all x1, blocking collectives, local(): lax.all_to_all(copies, 'zh', 0, 0, tiled=True)  26.7 us
    all_to_all x1, blocking collectives, local(): lax.all_to_all(parts.reshape(N_EP, slots // N_EP, 3 * group), EP, 0, 0, t...  16.8 us
    all_to_all x1, starting transfers between devices, local(): lax.all_to_all(slot_part.reshape(N_ZH, capacity, width), 'zh', 0, 0, tile...  13.2 us
    all_to_all x1, waiting for transfers between devices, local(): lax.all_to_all(slot_part.reshape(N_ZH, capacity, width), 'zh', 0, 0, tile...  10.4 us
    pallas_call x7, Pallas kernels, kernel_call(): pl.pallas_call(body, out_shape=outs, in_specs=[pl.BlockSpec(memory_space=...  9.07 us
    all_to_all x1, waiting for transfers between devices, local(): act = lax.all_to_all(copies, EP, 0, 0, tiled=True)  8.47 us
    all_to_all x1, waiting for transfers between devices, local(): lax.all_to_all(copies, 'yh', 0, 0, tiled=True).reshape(slots, width)  7.6 us
    all_to_all x1, starting transfers between devices, local(): lax.all_to_all(copies, 'yh', 0, 0, tiled=True).reshape(slots, width)  7.43 us
  transfers between devices with their start and end apart: 10, of which 5 were waited for; matrix products, arithmetic and copies ran while one was open for 2% of the time, Pallas kernels for 6%

profile of v4, /device:TPU:16, one launch (start us, length us, event | category | flops | bytes accessed | tf_op | source)
XLA Modules:
  0.0 139.4 jit_solution(3862995177735170902)
XLA Ops:
  0.6 2.1 %shard_map.102 = (bf16[6,16,768]{2,1,0:T(8,128)(2,1)}, bf16[16,128]{1,0:T(8,128)(2,1)}, bf16[3,112,768]{2,1,0:T(8,128)(2,1)}) custom-call(bf16[128,768]{1,0:T(8,128)(2,1)} %grad_ref.1, s32[4,128]{1,0:T(4,128)} %bitcast.35, f32[4,128]{1,0:T(4,128)} %bitcast.36, bf16[112,768]{1,0:T(8,128)(2,1)} %wg_hbm.1, bf16[112,768]{1,0:T(8,128)(2,1)} %wu_hbm.1, ...), custom_call_target="tpu_custom_call" | custom-call | tf_op jit(solution)/shard_map/pallas_call | solution.py:187
  2.8 26.7 %all_to_all.30 = bf16[6,16,768]{2,1,0:T(8,128)(2,1)S(1)} all-to-all(bf16[6,16,768]{2,1,0:T(8,128)(2,1)} %get-tuple-element.13), channel_id=1, replica_groups=mesh['yh'=4,'zh'=6,'zl'=2,'core'=2,'x'=4,'yl'=2] {'zh'}, dimensions={0} | all-to-all | bytes 294912 | tf_op jit(solution)/shard_map/all_to_all | solution.py:200
  29.5 3.6 %collective-permute-start = (bf16[3,112,768]{2,1,0:T(8,128)(2,1)}, bf16[3,112,768]{2,1,0:T(8,128)(2,1)S(1)}, u32[]{:S(2)}, u32[]{:S(2)}) collective-permute-start(bf16[3,112,768]{2,1,0:T(8,128)(2,1)} %get-tuple-element.15.own_ref), channel_id=1, source_target_pairs={{0,16},{16,0},{1,17},{17,1},{2,18},{18,2},{3,19},{19,3},{4,20},{20... | collective-permute-start | bytes 1548296 | tf_op jit(solution)/shard_map/ppermute | solution.py:203
  34.0 7.4 %all-to-all-start.1 = ((bf16[4,96,768]{2,1,0:T(8,128)(2,1)}), bf16[4,96,768]{2,1,0:T(8,128)(2,1)S(1)}, u32[]{:S(2)}, u32[]{:S(2)}) async-start(bf16[4,96,768]{2,1,0:T(8,128)(2,1)} %shard_map.103), calls=%async_computation.1 | async-start | bytes 1179648 | tf_op jit(solution)/shard_map/all_to_all | solution.py:206
  41.4 1.9 %collective-permute-start.1 = (bf16[3,112,768]{2,1,0:T(8,128)(2,1)S(1)}, bf16[3,112,768]{2,1,0:T(8,128)(2,1)S(1)}, u32[]{:S(2)}, u32[]{:S(2)}) collective-permute-start(bf16[3,112,768]{2,1,0:T(8,128)(2,1)S(1)} %copy-done.2), channel_id=1, source_target_pairs={{0,8},{8,0},{1,9},{9,1},{2,10},{10,2},{3,11},{11,3},{4,12},{12,4},... | collective-permute-start | bytes 1548296 | tf_op jit(solution)/shard_map/ppermute | solution.py:202
  43.3 2.4 %collective-permute-start.2 = (bf16[3,112,768]{2,1,0:T(8,128)(2,1)S(1)}, bf16[3,112,768]{2,1,0:T(8,128)(2,1)}, u32[]{:S(2)}, u32[]{:S(2)}) collective-permute-start(bf16[3,112,768]{2,1,0:T(8,128)(2,1)S(1)} %collective-permute-done.across_ref), channel_id=1, source_target_pairs={{0,8},{8,0},{1,9},{9,1},{2,10},{10,2},{3,11},{11,3},{4,12},{12,4},... | collective-permute-start | bytes 1548296 | tf_op jit(solution)/shard_map/ppermute | solution.py:205
  45.8 1.3 constant_dynamic-slice_fusion
  47.1 7.6 %all-to-all-done.1 = bf16[4,96,768]{2,1,0:T(8,128)(2,1)S(1)} async-done(((bf16[4,96,768]{2,1,0:T(8,128)(2,1)}), bf16[4,96,768]{2,1,0:T(8,128)(2,1)S(1)}, u32[]{:S(2)}, u32[]{:S(2)}) %all-to-all-start.1) | async-done | bytes 589856 | tf_op jit(solution)/shard_map/all_to_all | solution.py:206
  54.7 3.0 %shard_map.104 = (bf16[384,1344]{1,0:T(8,128)(2,1)S(1)}, bf16[896,768]{1,0:T(8,128)(2,1)}) custom-call(bf16[3,112,768]{2,1,0:T(8,128)(2,1)S(1)} %copy-done.2, bf16[3,112,768]{2,1,0:T(8,128)(2,1)S(1)} %collective-permute-done.across_ref, bf16[3,112,768]{2,1,0:T(8,128)(2,1)S(1)} %collective-permute-done.1.near_ref, ...), custom_call_target="tpu_custom_call" | custom-call | flops 792723456 | bytes 4000000 | tf_op jit(solution)/shard_map/pallas_call | solution.py:217
  57.7 16.8 %all_to_all.31.parts_ref = bf16[8,48,1344]{2,1,0:T(8,128)(2,1)S(1)} all-to-all(bf16[8,48,1344]{2,1,0:T(8,128)(2,1)S(1)} %bitcast.30), channel_id=1, replica_groups=mesh['yh'=4,'zh'=6,'zl'=2,'core'=2,'x'=4,'yl'=2] {'x','yl'}, dimensions={0} | all-to-all | bytes 2064384 | tf_op jit(solution)/shard_map/all_to_all | solution.py:227
  74.6 1.2 shard_map.105
  75.8 3.6 %all-to-all-start.3 = ((bf16[8,48,1344]{2,1,0:T(8,128)(2,1)}), bf16[8,48,1344]{2,1,0:T(8,128)(2,1)S(1)}, u32[]{:S(2)}, u32[]{:S(2)}) async-start(bf16[8,48,1344]{2,1,0:T(8,128)(2,1)} %shard_map.105), calls=%async_computation.3 | async-start | bytes 2162688 | tf_op jit(solution)/shard_map/all_to_all | solution.py:229
  79.4 3.8 %collective-permute-start.4 = (bf16[384,768]{1,0:T(8,128)(2,1)S(1)}, bf16[384,768]{1,0:T(8,128)(2,1)}, u32[]{:S(2)}, u32[]{:S(2)}) collective-permute-start(bf16[384,768]{1,0:T(8,128)(2,1)S(1)} %bitcast.25), channel_id=1, source_target_pairs={{0,16},{16,0},{1,17},{17,1},{2,18},{18,2},{3,19},{19,3},{4,20},{20... | collective-permute-start | bytes 1769480 | tf_op jit(solution)/shard_map/ppermute | solution.py:226
  83.1 8.5 %all-to-all-done.3 = bf16[8,48,1344]{2,1,0:T(8,128)(2,1)S(1)} async-done(((bf16[8,48,1344]{2,1,0:T(8,128)(2,1)}), bf16[8,48,1344]{2,1,0:T(8,128)(2,1)S(1)}, u32[]{:S(2)}, u32[]{:S(2)}) %all-to-all-start.3) | async-done | bytes 1032224 | tf_op jit(solution)/shard_map/all_to_all | solution.py:229
  91.6 1.2 shard_map.109
  92.8 4.4 %collective-permute-start.3 = (bf16[384,768]{1,0:T(8,128)(2,1)}, bf16[384,768]{1,0:T(8,128)(2,1)}, u32[]{:S(2)}, u32[]{:S(2)}) collective-permute-start(bf16[384,768]{1,0:T(8,128)(2,1)} %shard_map.109), channel_id=1, source_target_pairs={{0,16},{16,0},{1,17},{17,1},{2,18},{18,2},{3,19},{19,3},{4,20},{20... | collective-permute-start | bytes 1769480 | tf_op jit(solution)/shard_map/ppermute | solution.py:233
  97.2 1.8 %shard_map.106 = bf16[384,768]{1,0:T(8,128)(2,1)} custom-call(bf16[384,1344]{1,0:T(8,128)(2,1)S(1)} %bitcast.22, bf16[896,768]{1,0:T(8,128)(2,1)S(1)} %copy-done), custom_call_target="tpu_custom_call" | custom-call | flops 528482304 | bytes 3000000 | tf_op jit(solution)/shard_map/pallas_call | solution.py:234
  99.0 4.2 %all-to-all-start.4 = ((bf16[4,96,768]{2,1,0:T(8,128)(2,1)}), bf16[4,96,768]{2,1,0:T(8,128)(2,1)S(1)}, u32[]{:S(2)}, u32[]{:S(2)}) async-start(bf16[4,96,768]{2,1,0:T(8,128)(2,1)} %bitcast.32), calls=%async_computation.4 | async-start | bytes 1179648 | tf_op jit(solution)/shard_map/all_to_all | solution.py:244
  104.1 2.3 %collective-permute-done.3.act_ref = bf16[384,768]{1,0:T(8,128)(2,1)} collective-permute-done((bf16[384,768]{1,0:T(8,128)(2,1)}, bf16[384,768]{1,0:T(8,128)(2,1)}, u32[]{:S(2)}, u32[]{:S(2)}) %collective-permute-start.3) | collective-permute-done | bytes 589856 | tf_op jit(solution)/shard_map/ppermute | solution.py:233
  106.4 3.2 %shard_map.111 = (f32[3,112,768]{2,1,0:T(8,128)}, bf16[3,112,768]{2,1,0:T(8,128)(2,1)}) custom-call(bf16[384,768]{1,0:T(8,128)(2,1)} %collective-permute-done.3.act_ref, bf16[384,768]{1,0:T(8,128)(2,1)S(1)} %bitcast.29, bf16[384,768]{1,0:T(8,128)(2,1)} %collective-permute-done.4.gathered_ref, f32[3,224,768]{2,1,0:T(8,128)S(1)} %shard_map.110.part_ref), custom_call_target="tpu_custom_call" | custom-call | flops 396361728 | bytes 3833856 | tf_op jit(solution)/shard_map/pallas_call | solution.py:29
  109.6 2.0 %collective-permute-start.5 = (bf16[3,112,768]{2,1,0:T(8,128)(2,1)}, bf16[3,112,768]{2,1,0:T(8,128)(2,1)S(1)}, u32[]{:S(2)}, u32[]{:S(2)}) collective-permute-start(bf16[3,112,768]{2,1,0:T(8,128)(2,1)} %get-tuple-element.21), channel_id=1, source_target_pairs={{0,8},{8,0},{1,9},{9,1},{2,10},{10,2},{3,11},{11,3},{4,12},{12,4},... | collective-permute-start | bytes 1548296 | tf_op jit(solution)/shard_map/ppermute | solution.py:257
  111.7 1.4 %all-to-all-done.4.parts_ref = bf16[4,96,768]{2,1,0:T(8,128)(2,1)S(1)} async-done(((bf16[4,96,768]{2,1,0:T(8,128)(2,1)}), bf16[4,96,768]{2,1,0:T(8,128)(2,1)S(1)}, u32[]{:S(2)}, u32[]{:S(2)}) %all-to-all-start.4) | async-done | bytes 589856 | tf_op jit(solution)/shard_map/all_to_all | solution.py:244
  113.8 13.2 %all-to-all-start.5 = ((bf16[6,16,768]{2,1,0:T(8,128)(2,1)}), bf16[6,16,768]{2,1,0:T(8,128)(2,1)S(1)}, u32[]{:S(2)}, u32[]{:S(2)}) async-start(bf16[6,16,768]{2,1,0:T(8,128)(2,1)} %bitcast.34), calls=%async_computation.5 | async-start | bytes 294912 | tf_op jit(solution)/shard_map/all_to_all | solution.py:259
  128.0 10.4 %all-to-all-done.5.parts_ref = bf16[6,16,768]{2,1,0:T(8,128)(2,1)S(1)} async-done(((bf16[6,16,768]{2,1,0:T(8,128)(2,1)}), bf16[6,16,768]{2,1,0:T(8,128)(2,1)S(1)}, u32[]{:S(2)}, u32[]{:S(2)}) %all-to-all-start.5) | async-done | bytes 147488 | tf_op jit(solution)/shard_map/all_to_all | solution.py:259
  (20 shorter events, 4.5 us)
Async XLA Ops:
  2.8 38.6 %copy-start.2 = (bf16[3,112,768]{2,1,0:T(8,128)(2,1)S(1)}, bf16[3,112,768]{2,1,0:T(8,128)(2,1)}, u32[]{:S(2)}) copy-start(bf16[3,112,768]{2,1,0:T(8,128)(2,1)} %get-tuple-element.15.own_ref) | copy-start | bytes 1548292
  29.5 13.8 %collective-permute-start = (bf16[3,112,768]{2,1,0:T(8,128)(2,1)}, bf16[3,112,768]{2,1,0:T(8,128)(2,1)S(1)}, u32[]{:S(2)}, u32[]{:S(2)}) collective-permute-start(bf16[3,112,768]{2,1,0:T(8,128)(2,1)} %get-tuple-element.15.own_ref), channel_id=1, source_target_pairs={{0,16},{16,0},{1,17},{17,1},{2,18},{18,2},{3,19},{19,3},{4,20},{20... | collective-permute-start | bytes 1548296 | tf_op jit(solution)/shard_map/ppermute | solution.py:203
  34.0 20.7 %all-to-all-start.1 = ((bf16[4,96,768]{2,1,0:T(8,128)(2,1)}), bf16[4,96,768]{2,1,0:T(8,128)(2,1)S(1)}, u32[]{:S(2)}, u32[]{:S(2)}) async-start(bf16[4,96,768]{2,1,0:T(8,128)(2,1)} %shard_map.103), calls=%async_computation.1 | async-start | bytes 1179648 | tf_op jit(solution)/shard_map/all_to_all | solution.py:206
  41.4 5.7 %collective-permute-start.1 = (bf16[3,112,768]{2,1,0:T(8,128)(2,1)S(1)}, bf16[3,112,768]{2,1,0:T(8,128)(2,1)S(1)}, u32[]{:S(2)}, u32[]{:S(2)}) collective-permute-start(bf16[3,112,768]{2,1,0:T(8,128)(2,1)S(1)} %copy-done.2), channel_id=1, source_target_pairs={{0,8},{8,0},{1,9},{9,1},{2,10},{10,2},{3,11},{11,3},{4,12},{12,4},... | collective-permute-start | bytes 1548296 | tf_op jit(solution)/shard_map/ppermute | solution.py:202
  43.3 11.4 %collective-permute-start.2 = (bf16[3,112,768]{2,1,0:T(8,128)(2,1)S(1)}, bf16[3,112,768]{2,1,0:T(8,128)(2,1)}, u32[]{:S(2)}, u32[]{:S(2)}) collective-permute-start(bf16[3,112,768]{2,1,0:T(8,128)(2,1)S(1)} %collective-permute-done.across_ref), channel_id=1, source_target_pairs={{0,8},{8,0},{1,9},{9,1},{2,10},{10,2},{3,11},{11,3},{4,12},{12,4},... | collective-permute-start | bytes 1548296 | tf_op jit(solution)/shard_map/ppermute | solution.py:205
  75.8 15.8 %all-to-all-start.3 = ((bf16[8,48,1344]{2,1,0:T(8,128)(2,1)}), bf16[8,48,1344]{2,1,0:T(8,128)(2,1)S(1)}, u32[]{:S(2)}, u32[]{:S(2)}) async-start(bf16[8,48,1344]{2,1,0:T(8,128)(2,1)} %shard_map.105), calls=%async_computation.3 | async-start | bytes 2162688 | tf_op jit(solution)/shard_map/all_to_all | solution.py:229
  79.4 24.8 %collective-permute-start.4 = (bf16[384,768]{1,0:T(8,128)(2,1)S(1)}, bf16[384,768]{1,0:T(8,128)(2,1)}, u32[]{:S(2)}, u32[]{:S(2)}) collective-permute-start(bf16[384,768]{1,0:T(8,128)(2,1)S(1)} %bitcast.25), channel_id=1, source_target_pairs={{0,16},{16,0},{1,17},{17,1},{2,18},{18,2},{3,19},{19,3},{4,20},{20... | collective-permute-start | bytes 1769480 | tf_op jit(solution)/shard_map/ppermute | solution.py:226
  91.6 5.6 %copy-start = (bf16[896,768]{1,0:T(8,128)(2,1)S(1)}, bf16[896,768]{1,0:T(8,128)(2,1)}, u32[]{:S(2)}) copy-start(bf16[896,768]{1,0:T(8,128)(2,1)} %get-tuple-element.18.w_ref) | copy-start | bytes 4128772
  92.8 13.7 %collective-permute-start.3 = (bf16[384,768]{1,0:T(8,128)(2,1)}, bf16[384,768]{1,0:T(8,128)(2,1)}, u32[]{:S(2)}, u32[]{:S(2)}) collective-permute-start(bf16[384,768]{1,0:T(8,128)(2,1)} %shard_map.109), channel_id=1, source_target_pairs={{0,16},{16,0},{1,17},{17,1},{2,18},{18,2},{3,19},{19,3},{4,20},{20... | collective-permute-start | bytes 1769480 | tf_op jit(solution)/shard_map/ppermute | solution.py:233
  99.0 14.1 %all-to-all-start.4 = ((bf16[4,96,768]{2,1,0:T(8,128)(2,1)}), bf16[4,96,768]{2,1,0:T(8,128)(2,1)S(1)}, u32[]{:S(2)}, u32[]{:S(2)}) async-start(bf16[4,96,768]{2,1,0:T(8,128)(2,1)} %bitcast.32), calls=%async_computation.4 | async-start | bytes 1179648 | tf_op jit(solution)/shard_map/all_to_all | solution.py:244
  109.6 17.4 %copy-start.4 = (f32[3,112,768]{2,1,0:T(8,128)S(1)}, f32[3,112,768]{2,1,0:T(8,128)}, u32[]{:S(2)}) copy-start(f32[3,112,768]{2,1,0:T(8,128)} %get-tuple-element.20) | copy-start | bytes 3096580
  109.6 17.4 %collective-permute-start.5 = (bf16[3,112,768]{2,1,0:T(8,128)(2,1)}, bf16[3,112,768]{2,1,0:T(8,128)(2,1)S(1)}, u32[]{:S(2)}, u32[]{:S(2)}) collective-permute-start(bf16[3,112,768]{2,1,0:T(8,128)(2,1)} %get-tuple-element.21), channel_id=1, source_target_pairs={{0,8},{8,0},{1,9},{9,1},{2,10},{10,2},{3,11},{11,3},{4,12},{12,4},... | collective-permute-start | bytes 1548296 | tf_op jit(solution)/shard_map/ppermute | solution.py:257
  113.8 24.6 %copy-start.1 = (bf16[128,768]{1,0:T(8,128)(2,1)S(1)}, bf16[128,768]{1,0:T(8,128)(2,1)}, u32[]{:S(2)}) copy-start(bf16[128,768]{1,0:T(8,128)(2,1)} %grad_ref.1) | copy-start | bytes 589828
  113.8 24.6 %copy-start.3 = (bf16[16,128]{1,0:T(8,128)(2,1)S(1)}, bf16[16,128]{1,0:T(8,128)(2,1)}, u32[]{:S(2)}) copy-start(bf16[16,128]{1,0:T(8,128)(2,1)} %get-tuple-element.19.placement_ref) | copy-start | bytes 12292
  113.8 24.6 %all-to-all-start.5 = ((bf16[6,16,768]{2,1,0:T(8,128)(2,1)}), bf16[6,16,768]{2,1,0:T(8,128)(2,1)S(1)}, u32[]{:S(2)}, u32[]{:S(2)}) async-start(bf16[6,16,768]{2,1,0:T(8,128)(2,1)} %bitcast.34), calls=%async_computation.5 | async-start | bytes 294912 | tf_op jit(solution)/shard_map/all_to_all | solution.py:259

commit v5 on v4

--- a/solution.py
+++ b/solution.py
@@ -93,17 +93,21 @@
         copies_ref[i] = value_ref[...]
 
 
-def pre_kernel(own_ref, across_ref, near_ref, diagonal_ref, saved_ref, gathered_ref, parts_ref, w_hbm, w_ref, sem):
+def pre_kernel(own_ref, across_ref, near_ref, diagonal_ref, saved_ref, gathered_ref, parts_ref, w_ref):
     units = own_ref.shape[1]
     group = 4 * units
     for k in range(3):
         for i, ref in enumerate((own_ref, across_ref, near_ref, diagonal_ref)):
             w_ref[k * group + i * units : k * group + (i + 1) * units] = ref[k]
-    store = pltpu.make_async_copy(w_ref.at[pl.ds(0, 2 * group)], w_hbm, sem.at[0])
-    store.start()
     parts_ref[:, : 2 * group] = dot(saved_ref[...], w_ref[: 2 * group], LANES).astype(BF16)
     parts_ref[:, 2 * group :] = dot(gathered_ref[...], w_ref[2 * group :], LANES).astype(BF16)
-    store.wait()
+
+
+def weights_kernel(own_ref, across_ref, near_ref, diagonal_ref, w_ref):
+    units = own_ref.shape[1]
+    for k in range(2):
+        for i, ref in enumerate((own_ref, across_ref, near_ref, diagonal_ref)):
+            w_ref[(4 * k + i) * units : (4 * k + i + 1) * units] = ref[k]
 
 
 def activation_kernel(parts_ref, copies_ref):
@@ -214,17 +218,19 @@
     saved_far = slots_of((1 - chip) * 2 + core)
 
     pieces = (own, across, near, diagonal)
-    parts, w_both = pl.pallas_call(
+    (parts,) = pl.pallas_call(
         pre_kernel,
-        out_shape=[array(slots, 3 * group), HBM((2 * group, width), BF16)],
+        out_shape=[array(slots, 3 * group)],
         in_specs=[pl.BlockSpec(memory_space=VMEM)] * 6,
-        out_specs=[pl.BlockSpec(memory_space=VMEM), pl.BlockSpec(memory_space=pl.ANY)],
-        scratch_shapes=[VMEM((3 * group, width), BF16), pltpu.SemaphoreType.DMA((1,))],
+        out_specs=[pl.BlockSpec(memory_space=VMEM)],
+        scratch_shapes=[VMEM((3 * group, width), BF16)],
         cost_estimate=pl.CostEstimate(flops=6 * slots * group * width, bytes_accessed=4000000, transcendentals=0),
         compiler_params=pltpu.CompilerParams(vmem_limit_bytes=24 * 1024 * 1024),
     )(*pieces, saved, gathered)
     gathered_far = lax.ppermute(gathered, "zl", SWAP)
     parts = lax.all_to_all(parts.reshape(N_EP, slots // N_EP, 3 * group), EP, 0, 0, tiled=True)
+    parts, pieces = lax.optimization_barrier((parts, pieces))
+    (w_both,) = kernel_call(weights_kernel, [array(2 * group, width)], 1000000, *pieces)
     (copies,) = kernel_call(activation_kernel, [array(*parts.shape)], 20 * parts.size, parts)
     act = lax.all_to_all(copies, EP, 0, 0, tiled=True)
     act = act.reshape(slots, 3 * group)

time: 140 us -> 140 us (level)
  the two profiles are of different devices: /device:TPU:16 before, /device:TPU:12 now
where the time goes in v5:
time: 140 us; the launch traced here: 139 us
  starting transfers between devices  46.5 us (33%)
  blocking collectives  40.8 us (29%)
  waiting for transfers between devices  32.4 us (23%)
  Pallas kernels  16.3 us (12%)
    all_to_all x1, blocking collectives, local(): lax.all_to_all(copies, 'zh', 0, 0, tiled=True)  26.7 us
    all_to_all x1, blocking collectives, local(): lax.all_to_all(parts.reshape(N_EP, slots // N_EP, 3 * group), EP, 0, 0, t...  14.1 us
    all_to_all x1, starting transfers between devices, local(): lax.all_to_all(slot_part.reshape(N_ZH, capacity, width), 'zh', 0, 0, tile...  12.6 us
    all_to_all x1, waiting for transfers between devices, local(): lax.all_to_all(slot_part.reshape(N_ZH, capacity, width), 'zh', 0, 0, tile...  10.7 us
    pallas_call x8, Pallas kernels, kernel_call(): pl.pallas_call(body, out_shape=outs, in_specs=[pl.BlockSpec(memory_space=...  10.3 us
    all_to_all x1, waiting for transfers between devices, local(): lax.all_to_all(copies, 'yh', 0, 0, tiled=True).reshape(slots, width)  8.51 us
    all_to_all x1, starting transfers between devices, local(): lax.all_to_all(slot_part.reshape(N_YH, N_ZH * capacity, width), 'yh', 0,...  6.88 us
    all_to_all x1, starting transfers between devices, local(): act = lax.all_to_all(copies, EP, 0, 0, tiled=True)  6.75 us
  transfers between devices with their start and end apart: 10, of which 6 were waited for; matrix products, arithmetic and copies ran while one was open for 2% of the time, Pallas kernels for 7%

profile of v5, /device:TPU:12, one launch (start us, length us, event | category | flops | bytes accessed | tf_op | source)
XLA Modules:
  0.0 139.2 jit_solution(10873816147123183549)
XLA Ops:
  0.6 2.1 %shard_map.102 = (bf16[6,16,768]{2,1,0:T(8,128)(2,1)}, bf16[16,128]{1,0:T(8,128)(2,1)}, bf16[3,112,768]{2,1,0:T(8,128)(2,1)}) custom-call(bf16[128,768]{1,0:T(8,128)(2,1)} %grad_ref.1, s32[4,128]{1,0:T(4,128)} %bitcast.35, f32[4,128]{1,0:T(4,128)} %bitcast.36, bf16[112,768]{1,0:T(8,128)(2,1)} %wg_hbm.1, bf16[112,768]{1,0:T(8,128)(2,1)} %wu_hbm.1, ...), custom_call_target="tpu_custom_call" | custom-call | tf_op jit(solution)/shard_map/pallas_call | solution.py:191
  2.8 26.7 %all_to_all.30 = bf16[6,16,768]{2,1,0:T(8,128)(2,1)S(1)} all-to-all(bf16[6,16,768]{2,1,0:T(8,128)(2,1)} %get-tuple-element.16), channel_id=1, replica_groups=mesh['yh'=4,'zh'=6,'zl'=2,'core'=2,'x'=4,'yl'=2] {'zh'}, dimensions={0} | all-to-all | bytes 294912 | tf_op jit(solution)/shard_map/all_to_all | solution.py:204
  29.5 3.6 %collective-permute-start = (bf16[3,112,768]{2,1,0:T(8,128)(2,1)}, bf16[3,112,768]{2,1,0:T(8,128)(2,1)S(1)}, u32[]{:S(2)}, u32[]{:S(2)}) collective-permute-start(bf16[3,112,768]{2,1,0:T(8,128)(2,1)} %get-tuple-element.21.own_ref), channel_id=1, source_target_pairs={{0,16},{16,0},{1,17},{17,1},{2,18},{18,2},{3,19},{19,3},{4,20},{20... | collective-permute-start | bytes 1548296 | tf_op jit(solution)/shard_map/ppermute | solution.py:207
  34.0 6.2 %all-to-all-start.1 = ((bf16[4,96,768]{2,1,0:T(8,128)(2,1)}), bf16[4,96,768]{2,1,0:T(8,128)(2,1)S(1)}, u32[]{:S(2)}, u32[]{:S(2)}) async-start(bf16[4,96,768]{2,1,0:T(8,128)(2,1)} %shard_map.103), calls=%async_computation.1 | async-start | bytes 1179648 | tf_op jit(solution)/shard_map/all_to_all | solution.py:210
  40.2 1.9 %collective-permute-start.1 = (bf16[3,112,768]{2,1,0:T(8,128)(2,1)S(1)}, bf16[3,112,768]{2,1,0:T(8,128)(2,1)S(1)}, u32[]{:S(2)}, u32[]{:S(2)}) collective-permute-start(bf16[3,112,768]{2,1,0:T(8,128)(2,1)S(1)} %copy-done), channel_id=1, source_target_pairs={{0,8},{8,0},{1,9},{9,1},{2,10},{10,2},{3,11},{11,3},{4,12},{12,4},... | collective-permute-start | bytes 1548296 | tf_op jit(solution)/shard_map/ppermute | solution.py:206
  42.3 2.2 %collective-permute-start.2 = (bf16[3,112,768]{2,1,0:T(8,128)(2,1)S(1)}, bf16[3,112,768]{2,1,0:T(8,128)(2,1)}, u32[]{:S(2)}, u32[]{:S(2)}) collective-permute-start(bf16[3,112,768]{2,1,0:T(8,128)(2,1)S(1)} %collective-permute-done.across_ref), channel_id=1, source_target_pairs={{0,8},{8,0},{1,9},{9,1},{2,10},{10,2},{3,11},{11,3},{4,12},{12,4},... | collective-permute-start | bytes 1548296 | tf_op jit(solution)/shard_map/ppermute | solution.py:209
  44.5 1.3 constant_dynamic-slice_fusion
  45.9 8.5 %all-to-all-done.1 = bf16[4,96,768]{2,1,0:T(8,128)(2,1)S(1)} async-done(((bf16[4,96,768]{2,1,0:T(8,128)(2,1)}), bf16[4,96,768]{2,1,0:T(8,128)(2,1)S(1)}, u32[]{:S(2)}, u32[]{:S(2)}) %all-to-all-start.1) | async-done | bytes 589856 | tf_op jit(solution)/shard_map/all_to_all | solution.py:210
  54.4 2.1 %shard_map.104 = bf16[384,1344]{1,0:T(8,128)(2,1)S(1)} custom-call(bf16[3,112,768]{2,1,0:T(8,128)(2,1)S(1)} %copy-done, bf16[3,112,768]{2,1,0:T(8,128)(2,1)S(1)} %collective-permute-done.across_ref, bf16[3,112,768]{2,1,0:T(8,128)(2,1)S(1)} %collective-permute-done.1.near_ref, bf16[3,112,768]{2,1,0:T(8,128)(2,1)} %collective-permute-done.2.diagonal_ref, ...), custom_call_target="tpu_custom_call" | custom-call | flops 792723456 | bytes 4000000 | tf_op jit(solution)/shard_map/pallas_call | solution.py:221
  56.6 14.1 %all_to_all.31.parts_ref = bf16[8,48,1344]{2,1,0:T(8,128)(2,1)S(1)} all-to-all(bf16[8,48,1344]{2,1,0:T(8,128)(2,1)S(1)} %bitcast.29), channel_id=1, replica_groups=mesh['yh'=4,'zh'=6,'zl'=2,'core'=2,'x'=4,'yl'=2] {'x','yl'}, dimensions={0} | all-to-all | bytes 2064384 | tf_op jit(solution)/shard_map/all_to_all | solution.py:231
  70.7 1.3 shard_map.105
  72.0 6.7 %all-to-all-start.3 = ((bf16[8,48,1344]{2,1,0:T(8,128)(2,1)}), bf16[8,48,1344]{2,1,0:T(8,128)(2,1)S(1)}, u32[]{:S(2)}, u32[]{:S(2)}) async-start(bf16[8,48,1344]{2,1,0:T(8,128)(2,1)} %shard_map.105), calls=%async_computation.3 | async-start | bytes 2162688 | tf_op jit(solution)/shard_map/all_to_all | solution.py:235
  78.7 2.1 %collective-permute-start.4 = (bf16[384,768]{1,0:T(8,128)(2,1)S(1)}, bf16[384,768]{1,0:T(8,128)(2,1)}, u32[]{:S(2)}, u32[]{:S(2)}) collective-permute-start(bf16[384,768]{1,0:T(8,128)(2,1)S(1)} %bitcast.25), channel_id=1, source_target_pairs={{0,16},{16,0},{1,17},{17,1},{2,18},{18,2},{3,19},{19,3},{4,20},{20... | collective-permute-start | bytes 1769480 | tf_op jit(solution)/shard_map/ppermute | solution.py:230
  80.9 6.0 %all-to-all-done.3 = bf16[8,48,1344]{2,1,0:T(8,128)(2,1)S(1)} async-done(((bf16[8,48,1344]{2,1,0:T(8,128)(2,1)}), bf16[8,48,1344]{2,1,0:T(8,128)(2,1)S(1)}, u32[]{:S(2)}, u32[]{:S(2)}) %all-to-all-start.3) | async-done | bytes 1032224 | tf_op jit(solution)/shard_map/all_to_all | solution.py:235
  86.9 1.2 shard_map.110
  88.0 2.1 %collective-permute-start.3 = (bf16[384,768]{1,0:T(8,128)(2,1)}, bf16[384,768]{1,0:T(8,128)(2,1)}, u32[]{:S(2)}, u32[]{:S(2)}) collective-permute-start(bf16[384,768]{1,0:T(8,128)(2,1)} %shard_map.110), channel_id=1, source_target_pairs={{0,16},{16,0},{1,17},{17,1},{2,18},{18,2},{3,19},{19,3},{4,20},{20... | collective-permute-start | bytes 1769480 | tf_op jit(solution)/shard_map/ppermute | solution.py:239
  90.2 1.1 shard_map.106.w_ref
  91.3 1.8 %shard_map.107 = bf16[384,768]{1,0:T(8,128)(2,1)} custom-call(bf16[384,1344]{1,0:T(8,128)(2,1)S(1)} %bitcast.22, bf16[896,768]{1,0:T(8,128)(2,1)S(1)} %shard_map.106.w_ref), custom_call_target="tpu_custom_call" | custom-call | flops 528482304 | bytes 3000000 | tf_op jit(solution)/shard_map/pallas_call | solution.py:240
  93.1 6.9 %all-to-all-start.4 = ((bf16[4,96,768]{2,1,0:T(8,128)(2,1)}), bf16[4,96,768]{2,1,0:T(8,128)(2,1)S(1)}, u32[]{:S(2)}, u32[]{:S(2)}) async-start(bf16[4,96,768]{2,1,0:T(8,128)(2,1)} %bitcast.32), calls=%async_computation.4 | async-start | bytes 1179648 | tf_op jit(solution)/shard_map/all_to_all | solution.py:250
  102.0 3.2 %shard_map.112 = (f32[3,112,768]{2,1,0:T(8,128)}, bf16[3,112,768]{2,1,0:T(8,128)(2,1)}) custom-call(bf16[384,768]{1,0:T(8,128)(2,1)} %collective-permute-done.3.act_ref, bf16[384,768]{1,0:T(8,128)(2,1)S(1)} %bitcast.30, bf16[384,768]{1,0:T(8,128)(2,1)} %collective-permute-done.4.gathered_ref, f32[3,224,768]{2,1,0:T(8,128)S(1)} %shard_map.111.part_ref), custom_call_target="tpu_custom_call" | custom-call | flops 396361728 | bytes 3833856 | tf_op jit(solution)/shard_map/pallas_call | solution.py:29
  105.2 2.0 %collective-permute-start.5 = (bf16[3,112,768]{2,1,0:T(8,128)(2,1)}, bf16[3,112,768]{2,1,0:T(8,128)(2,1)S(1)}, u32[]{:S(2)}, u32[]{:S(2)}) collective-permute-start(bf16[3,112,768]{2,1,0:T(8,128)(2,1)} %get-tuple-element.27), channel_id=1, source_target_pairs={{0,8},{8,0},{1,9},{9,1},{2,10},{10,2},{3,11},{11,3},{4,12},{12,4},... | collective-permute-start | bytes 1548296 | tf_op jit(solution)/shard_map/ppermute | solution.py:263
  107.2 6.0 %all-to-all-done.4.parts_ref = bf16[4,96,768]{2,1,0:T(8,128)(2,1)S(1)} async-done(((bf16[4,96,768]{2,1,0:T(8,128)(2,1)}), bf16[4,96,768]{2,1,0:T(8,128)(2,1)S(1)}, u32[]{:S(2)}, u32[]{:S(2)}) %all-to-all-start.4) | async-done | bytes 589856 | tf_op jit(solution)/shard_map/all_to_all | solution.py:250
  113.9 12.6 %all-to-all-start.5 = ((bf16[6,16,768]{2,1,0:T(8,128)(2,1)}), bf16[6,16,768]{2,1,0:T(8,128)(2,1)S(1)}, u32[]{:S(2)}, u32[]{:S(2)}) async-start(bf16[6,16,768]{2,1,0:T(8,128)(2,1)} %bitcast.34), calls=%async_computation.5 | async-start | bytes 294912 | tf_op jit(solution)/shard_map/all_to_all | solution.py:265
  127.5 10.7 %all-to-all-done.5.parts_ref = bf16[6,16,768]{2,1,0:T(8,128)(2,1)S(1)} async-done(((bf16[6,16,768]{2,1,0:T(8,128)(2,1)}), bf16[6,16,768]{2,1,0:T(8,128)(2,1)S(1)}, u32[]{:S(2)}, u32[]{:S(2)}) %all-to-all-start.5) | async-done | bytes 147488 | tf_op jit(solution)/shard_map/all_to_all | solution.py:265
  (27 shorter events, 5.7 us)
Async XLA Ops:
  2.8 37.4 %copy-start = (bf16[3,112,768]{2,1,0:T(8,128)(2,1)S(1)}, bf16[3,112,768]{2,1,0:T(8,128)(2,1)}, u32[]{:S(2)}) copy-start(bf16[3,112,768]{2,1,0:T(8,128)(2,1)} %get-tuple-element.21.own_ref) | copy-start | bytes 1548292
  29.5 12.8 %collective-permute-start = (bf16[3,112,768]{2,1,0:T(8,128)(2,1)}, bf16[3,112,768]{2,1,0:T(8,128)(2,1)S(1)}, u32[]{:S(2)}, u32[]{:S(2)}) collective-permute-start(bf16[3,112,768]{2,1,0:T(8,128)(2,1)} %get-tuple-element.21.own_ref), channel_id=1, source_target_pairs={{0,16},{16,0},{1,17},{17,1},{2,18},{18,2},{3,19},{19,3},{4,20},{20... | collective-permute-start | bytes 1548296 | tf_op jit(solution)/shard_map/ppermute | solution.py:207
  34.0 20.4 %all-to-all-start.1 = ((bf16[4,96,768]{2,1,0:T(8,128)(2,1)}), bf16[4,96,768]{2,1,0:T(8,128)(2,1)S(1)}, u32[]{:S(2)}, u32[]{:S(2)}) async-start(bf16[4,96,768]{2,1,0:T(8,128)(2,1)} %shard_map.103), calls=%async_computation.1 | async-start | bytes 1179648 | tf_op jit(solution)/shard_map/all_to_all | solution.py:210
  40.2 5.7 %collective-permute-start.1 = (bf16[3,112,768]{2,1,0:T(8,128)(2,1)S(1)}, bf16[3,112,768]{2,1,0:T(8,128)(2,1)S(1)}, u32[]{:S(2)}, u32[]{:S(2)}) collective-permute-start(bf16[3,112,768]{2,1,0:T(8,128)(2,1)S(1)} %copy-done), channel_id=1, source_target_pairs={{0,8},{8,0},{1,9},{9,1},{2,10},{10,2},{3,11},{11,3},{4,12},{12,4},... | collective-permute-start | bytes 1548296 | tf_op jit(solution)/shard_map/ppermute | solution.py:206
  42.3 14.3 %copy-start.1 = (bf16[3,112,768]{2,1,0:T(8,128)(2,1)}, bf16[3,112,768]{2,1,0:T(8,128)(2,1)S(1)}, u32[]{:S(2)}) copy-start(bf16[3,112,768]{2,1,0:T(8,128)(2,1)S(1)} %collective-permute-done.across_ref) | copy-start | bytes 1548292
  42.3 12.1 %collective-permute-start.2 = (bf16[3,112,768]{2,1,0:T(8,128)(2,1)S(1)}, bf16[3,112,768]{2,1,0:T(8,128)(2,1)}, u32[]{:S(2)}, u32[]{:S(2)}) collective-permute-start(bf16[3,112,768]{2,1,0:T(8,128)(2,1)S(1)} %collective-permute-done.across_ref), channel_id=1, source_target_pairs={{0,8},{8,0},{1,9},{9,1},{2,10},{10,2},{3,11},{11,3},{4,12},{12,4},... | collective-permute-start | bytes 1548296 | tf_op jit(solution)/shard_map/ppermute | solution.py:209
  45.9 10.7 %copy-start.3 = (bf16[3,112,768]{2,1,0:T(8,128)(2,1)}, bf16[3,112,768]{2,1,0:T(8,128)(2,1)S(1)}, u32[]{:S(2)}) copy-start(bf16[3,112,768]{2,1,0:T(8,128)(2,1)S(1)} %collective-permute-done.1.near_ref) | copy-start | bytes 1548292
  72.0 14.9 %all-to-all-start.3 = ((bf16[8,48,1344]{2,1,0:T(8,128)(2,1)}), bf16[8,48,1344]{2,1,0:T(8,128)(2,1)S(1)}, u32[]{:S(2)}, u32[]{:S(2)}) async-start(bf16[8,48,1344]{2,1,0:T(8,128)(2,1)} %shard_map.105), calls=%async_computation.3 | async-start | bytes 2162688 | tf_op jit(solution)/shard_map/all_to_all | solution.py:235
  78.7 22.3 %collective-permute-start.4 = (bf16[384,768]{1,0:T(8,128)(2,1)S(1)}, bf16[384,768]{1,0:T(8,128)(2,1)}, u32[]{:S(2)}, u32[]{:S(2)}) collective-permute-start(bf16[384,768]{1,0:T(8,128)(2,1)S(1)} %bitcast.25), channel_id=1, source_target_pairs={{0,16},{16,0},{1,17},{17,1},{2,18},{18,2},{3,19},{19,3},{4,20},{20... | collective-permute-start | bytes 1769480 | tf_op jit(solution)/shard_map/ppermute | solution.py:230
  86.9 3.3 %copy-start.2 = (bf16[3,112,768]{2,1,0:T(8,128)(2,1)S(1)}, bf16[3,112,768]{2,1,0:T(8,128)(2,1)}, u32[]{:S(2)}) copy-start(bf16[3,112,768]{2,1,0:T(8,128)(2,1)} %copy-done.1) | copy-start | bytes 1548292
  86.9 3.3 %copy-start.4 = (bf16[3,112,768]{2,1,0:T(8,128)(2,1)S(1)}, bf16[3,112,768]{2,1,0:T(8,128)(2,1)}, u32[]{:S(2)}) copy-start(bf16[3,112,768]{2,1,0:T(8,128)(2,1)} %copy-done.3) | copy-start | bytes 1548292
  88.0 13.9 %collective-permute-start.3 = (bf16[384,768]{1,0:T(8,128)(2,1)}, bf16[384,768]{1,0:T(8,128)(2,1)}, u32[]{:S(2)}, u32[]{:S(2)}) collective-permute-start(bf16[384,768]{1,0:T(8,128)(2,1)} %shard_map.110), channel_id=1, source_target_pairs={{0,16},{16,0},{1,17},{17,1},{2,18},{18,2},{3,19},{19,3},{4,20},{20... | collective-permute-start | bytes 1769480 | tf_op jit(solution)/shard_map/ppermute | solution.py:239
  93.1 20.1 %all-to-all-start.4 = ((bf16[4,96,768]{2,1,0:T(8,128)(2,1)}), bf16[4,96,768]{2,1,0:T(8,128)(2,1)S(1)}, u32[]{:S(2)}, u32[]{:S(2)}) async-start(bf16[4,96,768]{2,1,0:T(8,128)(2,1)} %bitcast.32), calls=%async_computation.4 | async-start | bytes 1179648 | tf_op jit(solution)/shard_map/all_to_all | solution.py:250
  105.2 21.4 %copy-start.7 = (f32[3,112,768]{2,1,0:T(8,128)S(1)}, f32[3,112,768]{2,1,0:T(8,128)}, u32[]{:S(2)}) copy-start(f32[3,112,768]{2,1,0:T(8,128)} %get-tuple-element.26) | copy-start | bytes 3096580
  105.2 21.4 %collective-permute-start.5 = (bf16[3,112,768]{2,1,0:T(8,128)(2,1)}, bf16[3,112,768]{2,1,0:T(8,128)(2,1)S(1)}, u32[]{:S(2)}, u32[]{:S(2)}) collective-permute-start(bf16[3,112,768]{2,1,0:T(8,128)(2,1)} %get-tuple-element.27), channel_id=1, source_target_pairs={{0,8},{8,0},{1,9},{9,1},{2,10},{10,2},{3,11},{11,3},{4,12},{12,4},... | collective-permute-start | bytes 1548296 | tf_op jit(solution)/shard_map/ppermute | solution.py:263
  113.9 24.4 %copy-start.5 = (bf16[128,768]{1,0:T(8,128)(2,1)S(1)}, bf16[128,768]{1,0:T(8,128)(2,1)}, u32[]{:S(2)}) copy-start(bf16[128,768]{1,0:T(8,128)(2,1)} %grad_ref.1) | copy-start | bytes 589828
  113.9 24.4 %copy-start.6 = (bf16[16,128]{1,0:T(8,128)(2,1)S(1)}, bf16[16,128]{1,0:T(8,128)(2,1)}, u32[]{:S(2)}) copy-start(bf16[16,128]{1,0:T(8,128)(2,1)} %get-tuple-element.25.placement_ref) | copy-start | bytes 12292
  113.9 24.3 %all-to-all-start.5 = ((bf16[6,16,768]{2,1,0:T(8,128)(2,1)}), bf16[6,16,768]{2,1,0:T(8,128)(2,1)S(1)}, u32[]{:S(2)}, u32[]{:S(2)}) async-start(bf16[6,16,768]{2,1,0:T(8,128)(2,1)} %bitcast.34), calls=%async_computation.5 | async-start | bytes 294912 | tf_op jit(solution)/shard_map/all_to_all | solution.py:265

commit v6 on v5

--- a/solution.py
+++ b/solution.py
@@ -139,7 +139,8 @@
     sent_ref[...] = jnp.concatenate(columns, axis=1)
 
 
-def slot_kernel(act_ref, w_ref, slot_hbm, slot_ref, sems):
+def slot_kernel(act_ref, own_ref, across_ref, near_ref, diagonal_ref, slot_hbm, w_ref, slot_ref, sems):
+    weights_kernel(own_ref, across_ref, near_ref, diagonal_ref, w_ref)
     stores = []
     rows = act_ref.shape[0] // N_YH
     for i in range(N_YH):
@@ -230,7 +231,6 @@
     gathered_far = lax.ppermute(gathered, "zl", SWAP)
     parts = lax.all_to_all(parts.reshape(N_EP, slots // N_EP, 3 * group), EP, 0, 0, tiled=True)
     parts, pieces = lax.optimization_barrier((parts, pieces))
-    (w_both,) = kernel_call(weights_kernel, [array(2 * group, width)], 1000000, *pieces)
     (copies,) = kernel_call(activation_kernel, [array(*parts.shape)], 20 * parts.size, parts)
     act = lax.all_to_all(copies, EP, 0, 0, tiled=True)
     act = act.reshape(slots, 3 * group)
@@ -240,12 +240,12 @@
     slot_part = pl.pallas_call(
         slot_kernel,
         out_shape=HBM((slots, width), BF16),
-        in_specs=[pl.BlockSpec(memory_space=VMEM)] * 2,
+        in_specs=[pl.BlockSpec(memory_space=VMEM)] * 5,
         out_specs=pl.BlockSpec(memory_space=pl.ANY),
-        scratch_shapes=[VMEM((slots, width), BF16), pltpu.SemaphoreType.DMA((N_YH,))],
+        scratch_shapes=[VMEM((2 * group, width), BF16), VMEM((slots, width), BF16), pltpu.SemaphoreType.DMA((N_YH,))],
         cost_estimate=pl.CostEstimate(flops=4 * slots * group * width, bytes_accessed=3000000, transcendentals=0),
         compiler_params=pltpu.CompilerParams(vmem_limit_bytes=24 * 1024 * 1024),
-    )(act, w_both)
+    )(act, *pieces)
 
     slot_part = lax.all_to_all(slot_part.reshape(N_YH, N_ZH * capacity, width), "yh", 0, 0, tiled=True)
     (part,) = kernel_call(

time: 140 us -> 141 us (level)
  the two profiles are of different devices: /device:TPU:12 before, /device:TPU:16 now
where the time goes in v6:
time: 141 us; the launch traced here: 140 us
  starting transfers between devices  46.4 us (33%)
  blocking collectives  43.5 us (31%)
  waiting for transfers between devices  30.3 us (21%)
  Pallas kernels  16.2 us (11%)
    all_to_all x1, blocking collectives, local(): lax.all_to_all(copies, 'zh', 0, 0, tiled=True)  26.7 us
    all_to_all x1, blocking collectives, local(): lax.all_to_all(parts.reshape(N_EP, slots // N_EP, 3 * group), EP, 0, 0, t...  16.8 us
    all_to_all x1, starting transfers between devices, local(): lax.all_to_all(slot_part.reshape(N_ZH, capacity, width), 'zh', 0, 0, tile...  13.1 us
    all_to_all x1, waiting for transfers between devices, local(): lax.all_to_all(slot_part.reshape(N_ZH, capacity, width), 'zh', 0, 0, tile...  10.6 us
    pallas_call x7, Pallas kernels, kernel_call(): pl.pallas_call(body, out_shape=outs, in_specs=[pl.BlockSpec(memory_space=...  9.1 us
    all_to_all x1, waiting for transfers between devices, local(): act = lax.all_to_all(copies, EP, 0, 0, tiled=True)  8.47 us
    all_to_all x1, waiting for transfers between devices, local(): lax.all_to_all(copies, 'yh', 0, 0, tiled=True).reshape(slots, width)  7.58 us
    all_to_all x1, starting transfers between devices, local(): lax.all_to_all(copies, 'yh', 0, 0, tiled=True).reshape(slots, width)  7.43 us
  transfers between devices with their start and end apart: 10, of which 5 were waited for; matrix products, arithmetic and copies ran while one was open for 2% of the time, Pallas kernels for 7%

profile of v6, /device:TPU:16, one launch (start us, length us, event | category | flops | bytes accessed | tf_op | source)
XLA Modules:
  0.0 139.6 jit_solution(12729105274877741287)
XLA Ops:
  0.6 2.1 %shard_map.102 = (bf16[6,16,768]{2,1,0:T(8,128)(2,1)}, bf16[16,128]{1,0:T(8,128)(2,1)}, bf16[3,112,768]{2,1,0:T(8,128)(2,1)}) custom-call(bf16[128,768]{1,0:T(8,128)(2,1)} %grad_ref.1, s32[4,128]{1,0:T(4,128)} %bitcast.35, f32[4,128]{1,0:T(4,128)} %bitcast.36, bf16[112,768]{1,0:T(8,128)(2,1)} %wg_hbm.1, bf16[112,768]{1,0:T(8,128)(2,1)} %wu_hbm.1, ...), custom_call_target="tpu_custom_call" | custom-call | tf_op jit(solution)/shard_map/pallas_call | solution.py:192
  2.8 26.7 %all_to_all.30 = bf16[6,16,768]{2,1,0:T(8,128)(2,1)S(1)} all-to-all(bf16[6,16,768]{2,1,0:T(8,128)(2,1)} %get-tuple-element.16), channel_id=1, replica_groups=mesh['yh'=4,'zh'=6,'zl'=2,'core'=2,'x'=4,'yl'=2] {'zh'}, dimensions={0} | all-to-all | bytes 294912 | tf_op jit(solution)/shard_map/all_to_all | solution.py:205
  29.5 3.6 %collective-permute-start = (bf16[3,112,768]{2,1,0:T(8,128)(2,1)}, bf16[3,112,768]{2,1,0:T(8,128)(2,1)S(1)}, u32[]{:S(2)}, u32[]{:S(2)}) collective-permute-start(bf16[3,112,768]{2,1,0:T(8,128)(2,1)} %get-tuple-element.21.own_ref), channel_id=1, source_target_pairs={{0,16},{16,0},{1,17},{17,1},{2,18},{18,2},{3,19},{19,3},{4,20},{20... | collective-permute-start | bytes 1548296 | tf_op jit(solution)/shard_map/ppermute | solution.py:208
  34.0 7.4 %all-to-all-start.1 = ((bf16[4,96,768]{2,1,0:T(8,128)(2,1)}), bf16[4,96,768]{2,1,0:T(8,128)(2,1)S(1)}, u32[]{:S(2)}, u32[]{:S(2)}) async-start(bf16[4,96,768]{2,1,0:T(8,128)(2,1)} %shard_map.103), calls=%async_computation.1 | async-start | bytes 1179648 | tf_op jit(solution)/shard_map/all_to_all | solution.py:211
  41.4 1.9 %collective-permute-start.1 = (bf16[3,112,768]{2,1,0:T(8,128)(2,1)S(1)}, bf16[3,112,768]{2,1,0:T(8,128)(2,1)S(1)}, u32[]{:S(2)}, u32[]{:S(2)}) collective-permute-start(bf16[3,112,768]{2,1,0:T(8,128)(2,1)S(1)} %copy-done), channel_id=1, source_target_pairs={{0,8},{8,0},{1,9},{9,1},{2,10},{10,2},{3,11},{11,3},{4,12},{12,4},... | collective-permute-start | bytes 1548296 | tf_op jit(solution)/shard_map/ppermute | solution.py:207
  43.4 2.4 %collective-permute-start.2 = (bf16[3,112,768]{2,1,0:T(8,128)(2,1)S(1)}, bf16[3,112,768]{2,1,0:T(8,128)(2,1)}, u32[]{:S(2)}, u32[]{:S(2)}) collective-permute-start(bf16[3,112,768]{2,1,0:T(8,128)(2,1)S(1)} %collective-permute-done.across_ref), channel_id=1, source_target_pairs={{0,8},{8,0},{1,9},{9,1},{2,10},{10,2},{3,11},{11,3},{4,12},{12,4},... | collective-permute-start | bytes 1548296 | tf_op jit(solution)/shard_map/ppermute | solution.py:210
  45.8 1.3 constant_dynamic-slice_fusion
  47.1 7.6 %all-to-all-done.1 = bf16[4,96,768]{2,1,0:T(8,128)(2,1)S(1)} async-done(((bf16[4,96,768]{2,1,0:T(8,128)(2,1)}), bf16[4,96,768]{2,1,0:T(8,128)(2,1)S(1)}, u32[]{:S(2)}, u32[]{:S(2)}) %all-to-all-start.1) | async-done | bytes 589856 | tf_op jit(solution)/shard_map/all_to_all | solution.py:211
  54.7 2.2 %shard_map.104 = bf16[384,1344]{1,0:T(8,128)(2,1)S(1)} custom-call(bf16[3,112,768]{2,1,0:T(8,128)(2,1)S(1)} %copy-done, bf16[3,112,768]{2,1,0:T(8,128)(2,1)S(1)} %collective-permute-done.across_ref, bf16[3,112,768]{2,1,0:T(8,128)(2,1)S(1)} %collective-permute-done.1.near_ref, bf16[3,112,768]{2,1,0:T(8,128)(2,1)} %collective-permute-done.2.diagonal_ref, ...), custom_call_target="tpu_custom_call" | custom-call | flops 792723456 | bytes 4000000 | tf_op jit(solution)/shard_map/pallas_call | solution.py:222
  56.9 16.8 %all_to_all.31.parts_ref = bf16[8,48,1344]{2,1,0:T(8,128)(2,1)S(1)} all-to-all(bf16[8,48,1344]{2,1,0:T(8,128)(2,1)S(1)} %bitcast.29), channel_id=1, replica_groups=mesh['yh'=4,'zh'=6,'zl'=2,'core'=2,'x'=4,'yl'=2] {'x','yl'}, dimensions={0} | all-to-all | bytes 2064384 | tf_op jit(solution)/shard_map/all_to_all | solution.py:232
  73.7 1.2 shard_map.105
  74.9 3.6 %all-to-all-start.3 = ((bf16[8,48,1344]{2,1,0:T(8,128)(2,1)}), bf16[8,48,1344]{2,1,0:T(8,128)(2,1)S(1)}, u32[]{:S(2)}, u32[]{:S(2)}) async-start(bf16[8,48,1344]{2,1,0:T(8,128)(2,1)} %shard_map.105), calls=%async_computation.3 | async-start | bytes 2162688 | tf_op jit(solution)/shard_map/all_to_all | solution.py:235
  78.5 3.8 %collective-permute-start.4 = (bf16[384,768]{1,0:T(8,128)(2,1)S(1)}, bf16[384,768]{1,0:T(8,128)(2,1)}, u32[]{:S(2)}, u32[]{:S(2)}) collective-permute-start(bf16[384,768]{1,0:T(8,128)(2,1)S(1)} %bitcast.25), channel_id=1, source_target_pairs={{0,16},{16,0},{1,17},{17,1},{2,18},{18,2},{3,19},{19,3},{4,20},{20... | collective-permute-start | bytes 1769480 | tf_op jit(solution)/shard_map/ppermute | solution.py:231
  82.3 8.5 %all-to-all-done.3 = bf16[8,48,1344]{2,1,0:T(8,128)(2,1)S(1)} async-done(((bf16[8,48,1344]{2,1,0:T(8,128)(2,1)}), bf16[8,48,1344]{2,1,0:T(8,128)(2,1)S(1)}, u32[]{:S(2)}, u32[]{:S(2)}) %all-to-all-start.3) | async-done | bytes 1032224 | tf_op jit(solution)/shard_map/all_to_all | solution.py:235
  90.8 1.2 shard_map.109
  91.9 4.4 %collective-permute-start.3 = (bf16[384,768]{1,0:T(8,128)(2,1)}, bf16[384,768]{1,0:T(8,128)(2,1)}, u32[]{:S(2)}, u32[]{:S(2)}) collective-permute-start(bf16[384,768]{1,0:T(8,128)(2,1)} %shard_map.109), channel_id=1, source_target_pairs={{0,16},{16,0},{1,17},{17,1},{2,18},{18,2},{3,19},{19,3},{4,20},{20... | collective-permute-start | bytes 1769480 | tf_op jit(solution)/shard_map/ppermute | solution.py:239
  96.3 2.8 %shard_map.106 = bf16[384,768]{1,0:T(8,128)(2,1)} custom-call(bf16[384,1344]{1,0:T(8,128)(2,1)S(1)} %bitcast.22, bf16[3,112,768]{2,1,0:T(8,128)(2,1)S(1)} %copy-done, bf16[3,112,768]{2,1,0:T(8,128)(2,1)S(1)} %copy-done.2, bf16[3,112,768]{2,1,0:T(8,128)(2,1)S(1)} %copy-done.4, bf16[3,112,768]{2,1,0:T(8,128)(2,1)} %collective-permute-done.2.diagonal_ref), custom_call_target="tpu_custom_call" | custom-call | flops 528482304 | bytes 3000000 | tf_op jit(solution)/shard_map/pallas_call | solution.py:240
  99.2 4.2 %all-to-all-start.4 = ((bf16[4,96,768]{2,1,0:T(8,128)(2,1)}), bf16[4,96,768]{2,1,0:T(8,128)(2,1)S(1)}, u32[]{:S(2)}, u32[]{:S(2)}) async-start(bf16[4,96,768]{2,1,0:T(8,128)(2,1)} %bitcast.32), calls=%async_computation.4 | async-start | bytes 1179648 | tf_op jit(solution)/shard_map/all_to_all | solution.py:250
  104.4 1.2 collective-permute-done.3.act_ref
  105.6 3.2 %shard_map.111 = (f32[3,112,768]{2,1,0:T(8,128)}, bf16[3,112,768]{2,1,0:T(8,128)(2,1)}) custom-call(bf16[384,768]{1,0:T(8,128)(2,1)} %collective-permute-done.3.act_ref, bf16[384,768]{1,0:T(8,128)(2,1)S(1)} %bitcast.30, bf16[384,768]{1,0:T(8,128)(2,1)} %collective-permute-done.4.gathered_ref, f32[3,224,768]{2,1,0:T(8,128)S(1)} %shard_map.110.part_ref), custom_call_target="tpu_custom_call" | custom-call | flops 396361728 | bytes 3833856 | tf_op jit(solution)/shard_map/pallas_call | solution.py:29
  108.8 2.0 %collective-permute-start.5 = (bf16[3,112,768]{2,1,0:T(8,128)(2,1)}, bf16[3,112,768]{2,1,0:T(8,128)(2,1)S(1)}, u32[]{:S(2)}, u32[]{:S(2)}) collective-permute-start(bf16[3,112,768]{2,1,0:T(8,128)(2,1)} %get-tuple-element.27), channel_id=1, source_target_pairs={{0,8},{8,0},{1,9},{9,1},{2,10},{10,2},{3,11},{11,3},{4,12},{12,4},... | collective-permute-start | bytes 1548296 | tf_op jit(solution)/shard_map/ppermute | solution.py:263
  110.8 2.5 %all-to-all-done.4.parts_ref = bf16[4,96,768]{2,1,0:T(8,128)(2,1)S(1)} async-done(((bf16[4,96,768]{2,1,0:T(8,128)(2,1)}), bf16[4,96,768]{2,1,0:T(8,128)(2,1)S(1)}, u32[]{:S(2)}, u32[]{:S(2)}) %all-to-all-start.4) | async-done | bytes 589856 | tf_op jit(solution)/shard_map/all_to_all | solution.py:250
  114.1 13.1 %all-to-all-start.5 = ((bf16[6,16,768]{2,1,0:T(8,128)(2,1)}), bf16[6,16,768]{2,1,0:T(8,128)(2,1)S(1)}, u32[]{:S(2)}, u32[]{:S(2)}) async-start(bf16[6,16,768]{2,1,0:T(8,128)(2,1)} %bitcast.34), calls=%async_computation.5 | async-start | bytes 294912 | tf_op jit(solution)/shard_map/all_to_all | solution.py:265
  128.2 10.6 %all-to-all-done.5.parts_ref = bf16[6,16,768]{2,1,0:T(8,128)(2,1)S(1)} async-done(((bf16[6,16,768]{2,1,0:T(8,128)(2,1)}), bf16[6,16,768]{2,1,0:T(8,128)(2,1)S(1)}, u32[]{:S(2)}, u32[]{:S(2)}) %all-to-all-start.5) | async-done | bytes 147488 | tf_op jit(solution)/shard_map/all_to_all | solution.py:265
  (26 shorter events, 4.6 us)
Async XLA Ops:
  2.8 38.7 %copy-start = (bf16[3,112,768]{2,1,0:T(8,128)(2,1)S(1)}, bf16[3,112,768]{2,1,0:T(8,128)(2,1)}, u32[]{:S(2)}) copy-start(bf16[3,112,768]{2,1,0:T(8,128)(2,1)} %get-tuple-element.21.own_ref) | copy-start | bytes 1548292
  29.5 13.9 %collective-permute-start = (bf16[3,112,768]{2,1,0:T(8,128)(2,1)}, bf16[3,112,768]{2,1,0:T(8,128)(2,1)S(1)}, u32[]{:S(2)}, u32[]{:S(2)}) collective-permute-start(bf16[3,112,768]{2,1,0:T(8,128)(2,1)} %get-tuple-element.21.own_ref), channel_id=1, source_target_pairs={{0,16},{16,0},{1,17},{17,1},{2,18},{18,2},{3,19},{19,3},{4,20},{20... | collective-permute-start | bytes 1548296 | tf_op jit(solution)/shard_map/ppermute | solution.py:208
  34.0 20.7 %all-to-all-start.1 = ((bf16[4,96,768]{2,1,0:T(8,128)(2,1)}), bf16[4,96,768]{2,1,0:T(8,128)(2,1)S(1)}, u32[]{:S(2)}, u32[]{:S(2)}) async-start(bf16[4,96,768]{2,1,0:T(8,128)(2,1)} %shard_map.103), calls=%async_computation.1 | async-start | bytes 1179648 | tf_op jit(solution)/shard_map/all_to_all | solution.py:211
  41.4 5.7 %collective-permute-start.1 = (bf16[3,112,768]{2,1,0:T(8,128)(2,1)S(1)}, bf16[3,112,768]{2,1,0:T(8,128)(2,1)S(1)}, u32[]{:S(2)}, u32[]{:S(2)}) collective-permute-start(bf16[3,112,768]{2,1,0:T(8,128)(2,1)S(1)} %copy-done), channel_id=1, source_target_pairs={{0,8},{8,0},{1,9},{9,1},{2,10},{10,2},{3,11},{11,3},{4,12},{12,4},... | collective-permute-start | bytes 1548296 | tf_op jit(solution)/shard_map/ppermute | solution.py:207
  43.3 11.4 %copy-start.1 = (bf16[3,112,768]{2,1,0:T(8,128)(2,1)}, bf16[3,112,768]{2,1,0:T(8,128)(2,1)S(1)}, u32[]{:S(2)}) copy-start(bf16[3,112,768]{2,1,0:T(8,128)(2,1)S(1)} %collective-permute-done.across_ref) | copy-start | bytes 1548292
  43.4 11.4 %collective-permute-start.2 = (bf16[3,112,768]{2,1,0:T(8,128)(2,1)S(1)}, bf16[3,112,768]{2,1,0:T(8,128)(2,1)}, u32[]{:S(2)}, u32[]{:S(2)}) collective-permute-start(bf16[3,112,768]{2,1,0:T(8,128)(2,1)S(1)} %collective-permute-done.across_ref), channel_id=1, source_target_pairs={{0,8},{8,0},{1,9},{9,1},{2,10},{10,2},{3,11},{11,3},{4,12},{12,4},... | collective-permute-start | bytes 1548296 | tf_op jit(solution)/shard_map/ppermute | solution.py:210
  47.1 9.8 %copy-start.3 = (bf16[3,112,768]{2,1,0:T(8,128)(2,1)}, bf16[3,112,768]{2,1,0:T(8,128)(2,1)S(1)}, u32[]{:S(2)}) copy-start(bf16[3,112,768]{2,1,0:T(8,128)(2,1)S(1)} %collective-permute-done.1.near_ref) | copy-start | bytes 1548292
  74.9 15.8 %all-to-all-start.3 = ((bf16[8,48,1344]{2,1,0:T(8,128)(2,1)}), bf16[8,48,1344]{2,1,0:T(8,128)(2,1)S(1)}, u32[]{:S(2)}, u32[]{:S(2)}) async-start(bf16[8,48,1344]{2,1,0:T(8,128)(2,1)} %shard_map.105), calls=%async_computation.3 | async-start | bytes 2162688 | tf_op jit(solution)/shard_map/all_to_all | solution.py:235
  78.5 25.8 %collective-permute-start.4 = (bf16[384,768]{1,0:T(8,128)(2,1)S(1)}, bf16[384,768]{1,0:T(8,128)(2,1)}, u32[]{:S(2)}, u32[]{:S(2)}) collective-permute-start(bf16[384,768]{1,0:T(8,128)(2,1)S(1)} %bitcast.25), channel_id=1, source_target_pairs={{0,16},{16,0},{1,17},{17,1},{2,18},{18,2},{3,19},{19,3},{4,20},{20... | collective-permute-start | bytes 1769480 | tf_op jit(solution)/shard_map/ppermute | solution.py:231
  90.8 5.6 %copy-start.2 = (bf16[3,112,768]{2,1,0:T(8,128)(2,1)S(1)}, bf16[3,112,768]{2,1,0:T(8,128)(2,1)}, u32[]{:S(2)}) copy-start(bf16[3,112,768]{2,1,0:T(8,128)(2,1)} %copy-done.1) | copy-start | bytes 1548292
  90.8 5.6 %copy-start.4 = (bf16[3,112,768]{2,1,0:T(8,128)(2,1)S(1)}, bf16[3,112,768]{2,1,0:T(8,128)(2,1)}, u32[]{:S(2)}) copy-start(bf16[3,112,768]{2,1,0:T(8,128)(2,1)} %copy-done.3) | copy-start | bytes 1548292
  91.9 13.7 %collective-permute-start.3 = (bf16[384,768]{1,0:T(8,128)(2,1)}, bf16[384,768]{1,0:T(8,128)(2,1)}, u32[]{:S(2)}, u32[]{:S(2)}) collective-permute-start(bf16[384,768]{1,0:T(8,128)(2,1)} %shard_map.109), channel_id=1, source_target_pairs={{0,16},{16,0},{1,17},{17,1},{2,18},{18,2},{3,19},{19,3},{4,20},{20... | collective-permute-start | bytes 1769480 | tf_op jit(solution)/shard_map/ppermute | solution.py:239
  99.2 14.1 %all-to-all-start.4 = ((bf16[4,96,768]{2,1,0:T(8,128)(2,1)}), bf16[4,96,768]{2,1,0:T(8,128)(2,1)S(1)}, u32[]{:S(2)}, u32[]{:S(2)}) async-start(bf16[4,96,768]{2,1,0:T(8,128)(2,1)} %bitcast.32), calls=%async_computation.4 | async-start | bytes 1179648 | tf_op jit(solution)/shard_map/all_to_all | solution.py:250
  108.8 18.4 %copy-start.7 = (f32[3,112,768]{2,1,0:T(8,128)S(1)}, f32[3,112,768]{2,1,0:T(8,128)}, u32[]{:S(2)}) copy-start(f32[3,112,768]{2,1,0:T(8,128)} %get-tuple-element.26) | copy-start | bytes 3096580
  108.8 18.4 %collective-permute-start.5 = (bf16[3,112,768]{2,1,0:T(8,128)(2,1)}, bf16[3,112,768]{2,1,0:T(8,128)(2,1)S(1)}, u32[]{:S(2)}, u32[]{:S(2)}) collective-permute-start(bf16[3,112,768]{2,1,0:T(8,128)(2,1)} %get-tuple-element.27), channel_id=1, source_target_pairs={{0,8},{8,0},{1,9},{9,1},{2,10},{10,2},{3,11},{11,3},{4,12},{12,4},... | collective-permute-start | bytes 1548296 | tf_op jit(solution)/shard_map/ppermute | solution.py:263
  114.1 24.7 %all-to-all-start.5 = ((bf16[6,16,768]{2,1,0:T(8,128)(2,1)}), bf16[6,16,768]{2,1,0:T(8,128)(2,1)S(1)}, u32[]{:S(2)}, u32[]{:S(2)}) async-start(bf16[6,16,768]{2,1,0:T(8,128)(2,1)} %bitcast.34), calls=%async_computation.5 | async-start | bytes 294912 | tf_op jit(solution)/shard_map/all_to_all | solution.py:265
  127.2 11.6 %copy-start.5 = (bf16[128,768]{1,0:T(8,128)(2,1)S(1)}, bf16[128,768]{1,0:T(8,128)(2,1)}, u32[]{:S(2)}) copy-start(bf16[128,768]{1,0:T(8,128)(2,1)} %grad_ref.1) | copy-start | bytes 589828
  127.2 11.6 %copy-start.6 = (bf16[16,128]{1,0:T(8,128)(2,1)S(1)}, bf16[16,128]{1,0:T(8,128)(2,1)}, u32[]{:S(2)}) copy-start(bf16[16,128]{1,0:T(8,128)(2,1)} %get-tuple-element.25.placement_ref) | copy-start | bytes 12292
